TPU v7x, 32 devices: a whole 2x2x4 slice. The times are simulated.
32 devices in a mesh: expert: 4 (over z), hrow: 4 (over x, core), hcol: 2 (over y).
Axes of the slice: x: 2, y: 2, z: 4, core: 2. Of those that a mesh axis runs over, the one named last changes fastest.
Arguments:
- tokens: bfloat16 [256, 7168], P(('expert', 'hrow'), 'hcol')
- expert_ids: int32 [256, 8], P(('expert', 'hrow')), may hold values from 0 to 15, all different within a row; in each aligned block of 16 rows (0 to 15, 16 to 31, ...) at most 16 rows name the same one
- weight: bfloat16 [16, 256, 7168], P(('expert', 'hrow'), None, 'hcol'), may hold values from -6 to 6
- mask_bits: int32 [256, 224], P(None, 'hcol'), may hold values from -2147483648 to 2147483646, as said below
- damping: float32 [16, 7168], P(('expert', 'hrow'), 'hcol'), may hold values from 0.5 to 2
Outputs:
- new_weight: bfloat16 [16, 256, 7168], P(('expert', 'hrow'), None, 'hcol')
Inputs may be any that keep to these rules, and one draw needn't show every extreme that they name: `expert_ids`: each token names 8 different experts; among the 16 rows of one device (aligned blocks of rows) no expert is named more than 16 times, a bound that some block reaches. `mask_bits`: every bit of every word is a keep flag (1 keeps the entry, 0 prunes it).
All inputs are finite; a program needn't handle non-finite values.
Results may differ from a plain program's by a relative error of at most 0.0044.
Values may be sent and summed in bfloat16 or wider, within the bound.
A program may use at most 64 MiB of HBM per device.

v0:
```python
import jax
import jax.numpy as jnp
from jax import lax
from jax.sharding import PartitionSpec as P

ROWS_E = 128


ETA = 0.5


def unpack_bits(bits):
    bit_shifts = jnp.arange(32, dtype=jnp.int32)
    bit_flags = jnp.bitwise_and(jnp.right_shift(bits[:, :, None], bit_shifts[None, None, :]), 1)
    return bit_flags.reshape(bits.shape[0], bits.shape[1] * 32)


def route_rows(tokens, expert_ids, group_count, local_count):
    tok_count, top_count = expert_ids.shape
    expert_count = group_count * local_count
    capacity = 2 * tok_count * top_count // expert_count
    flat_ids = expert_ids.reshape(-1)
    one_hot = (flat_ids[:, None] == jnp.arange(expert_count, dtype=jnp.int32)[None, :]).astype(
        jnp.int32
    )
    prior_count = jnp.cumsum(one_hot, axis=0) - one_hot
    slot_index = jnp.sum(prior_count * one_hot, axis=1)
    group_of = flat_ids // local_count
    local_of = flat_ids % local_count
    target_slot = ((local_of * group_count + group_of) * capacity + slot_index).reshape(
        tok_count, top_count
    )
    slot_ids = jnp.arange(expert_count * capacity, dtype=jnp.int32)
    selector = jnp.any(slot_ids[:, None, None] == target_slot[None, :, :], axis=2).astype(
        jnp.bfloat16
    )
    packed = jnp.dot(selector, tokens, preferred_element_type=jnp.float32).astype(jnp.bfloat16)
    return packed.reshape(local_count, group_count, 1, capacity, tokens.shape[1])


def local(tokens, expert_ids, weight, mask_bits, damping):
    group_count = lax.axis_size(("expert", "hrow"))
    local_experts = weight.shape[0]
    feat_width = tokens.shape[1]
    slab_rows = weight.shape[1]
    packed = route_rows(tokens, expert_ids, group_count, local_experts)
    keep_flags = unpack_bits(mask_bits)
    keep_mask = keep_flags[None, :, :] == 1
    pruned = jnp.where(keep_mask, jnp.zeros_like(weight), weight)
    block = lax.all_to_all(packed, ("expert", "hrow"), split_axis=1, concat_axis=2, tiled=True)
    partials = jnp.einsum("esf,exgcf->exgcs", pruned, block, preferred_element_type=jnp.float32)
    slot_count = block.shape[1] * block.shape[2] * block.shape[3]
    routed = block.reshape(local_experts, slot_count, feat_width)
    partials = partials.reshape(local_experts, slot_count, slab_rows)
    projected = lax.psum(partials, "hcol").astype(jnp.bfloat16)
    comp_term = (
        jnp.einsum("ers,erf->esf", projected, routed, preferred_element_type=jnp.float32) / ROWS_E
    )
    diag_scale = (
        jnp.einsum("erf,erf->ef", routed, routed, preferred_element_type=jnp.float32) / ROWS_E
        + damping
    )
    updated = weight.astype(jnp.float32) + ETA * comp_term / diag_scale[:, None, :]
    return jnp.where(keep_mask, updated, jnp.float32(0.0)).astype(jnp.bfloat16)


def solution(mesh):
    in_specs = (
        P(("expert", "hrow"), "hcol"),
        P(("expert", "hrow"), None),
        P(("expert", "hrow"), None, "hcol"),
        P(None, "hcol"),
        P(("expert", "hrow"), "hcol"),
    )
    out_specs = P(("expert", "hrow"), None, "hcol")
    return jax.shard_map(local, mesh=mesh, in_specs=in_specs, out_specs=out_specs, check_vma=False)
```

profile of v0, /device:TPU:10, one launch (start us, length us, event | category | flops | bytes accessed | tf_op | source)
XLA Modules:
  0.0 70.3 jit_solution(17555118394924780134)
XLA Ops:
  0.0 0.0 copy-start
  0.0 0.0 copy-start.1
  0.0 0.8 %copy.17 = s32[16,8]{1,0:T(8,128)S(1)} copy(s32[16,8]{0,1:T(8,128)} %param.6) | data formatting | bytes 1024 | tf_op args[1]
  0.8 0.1 eq.44
  0.9 0.1 fusion.16
  1.0 0.2 reduce_window_sum.11
  1.2 0.2 select_reduce_fusion
  1.3 0.1 reduce_sum.12
  1.4 0.1 fusion.15
  1.6 0.0 copy-done
  1.6 1.9 %convolution_convert_fusion = bf16[256,3584]{1,0:T(8,128)(2,1)} fusion(pred[256,16]{0,1:T(8,128)(4,1)S(1)} %fusion.15, bf16[16,3584]{1,0:T(8,128)(2,1)S(1)} %copy-done), kind=kOutput, calls=%fused_computation.1 | convolution fusion | flops 30277632 | bytes 1953792 | tf_op jit(solution)/shard_map/dot_general | solution.py:37
  3.5 6.2 %all-to-all-start = ((bf16[1,16,1,16,3584]{4,3,2,0,1:T(8,128)(2,1)}), bf16[1,16,1,16,3584]{4,3,2,0,1:T(8,128)(2,1)S(1)}, u32[]{:S(2)}, u32[]{:S(2)}) async-start(bf16[1,16,1,16,3584]{4,3,2,0,1:T(8,128)(2,1)} %bitcast.35), calls=%async_computation | async-start | bytes 3670016 | tf_op jit(solution)/shard_map/all_to_all | solution.py:50
  9.7 0.0 copy-done.1
  9.7 2.1 %shift_right_arithmetic.27 = s32[256,112,32]{0,2,1:T(8,128)} broadcast(s32[256,112]{0,1:T(8,128)S(1)} %copy-done.1), dimensions={0,1} | broadcast | bytes 3784704 | tf_op jit(solution)/shard_map/shift_right_arithmetic | solution.py:14
  11.8 5.2 %copy.16 = s32[1,256,3584]{2,1,0:T(8,128)} copy(s32[1,256,3584]{1,2,0:T(8,128)} %bitcast.32) | data formatting | bytes 7340032 | tf_op jit(solution)/shard_map/shift_right_arithmetic | solution.py:14
  17.0 0.1 shift_right_arithmetic.30
  17.1 2.8 %and_compare_fusion = pred[1,256,3584]{2,1,0:T(32,128)(4,1)S(1)} fusion(s32[1,256,3584]{2,1,0:T(8,128)} %copy.16, s32[3584]{0:T(1024)S(1)} %shift_right_arithmetic.30), kind=kLoop, calls=%fused_computation.9 | loop fusion | flops 2752512 | bytes 4601856 | tf_op jit(solution)/shard_map/eq | solution.py:48
  19.8 0.0 copy-start.2
  19.8 31.5 %all-to-all-done = bf16[1,16,1,16,3584]{4,3,2,0,1:T(8,128)(2,1)S(1)} async-done(((bf16[1,16,1,16,3584]{4,3,2,0,1:T(8,128)(2,1)}), bf16[1,16,1,16,3584]{4,3,2,0,1:T(8,128)(2,1)S(1)}, u32[]{:S(2)}, u32[]{:S(2)}) %all-to-all-start) | async-done | bytes 1835040 | tf_op jit(solution)/shard_map/all_to_all | solution.py:50
  51.4 0.5 fusion.5
  51.9 2.2 %fusion.9 = f32[1,256,256]{2,1,0:T(8,128)S(1)} fusion(bf16[256,3584]{1,0:T(8,128)(2,1)S(1)} %bitcast.33, pred[1,256,3584]{2,1,0:T(32,128)(4,1)S(1)} %and_compare_fusion, bf16[1,256,3584]{2,1,0:T(8,128)(2,1)} %param.7), kind=kOutput, calls=%fused_computation.13 | convolution fusion | flops 470679552 | bytes 4849664 | tf_op jit(solution)/shard_map/esf,exgcf->exgcs/dot_general | solution.py:51
  54.1 12.2 %all-reduce.1 = bf16[1,256,256]{2,1,0:T(8,128)(2,1)S(1)} all-reduce(f32[1,256,256]{2,1,0:T(8,128)S(1)} %fusion.9), channel_id=1, replica_groups=mesh['expert'=4,'hrow'=4,'hcol'=2] {'hcol'}, use_global_device_ids=true, to_apply=%region_3.4 | all-reduce | flops 65536 | bytes 393216 | tf_op jit(solution)/shard_map/psum | solution.py:55
  66.3 0.0 copy-done.2
  66.4 3.9 %fusion.4 = bf16[1,256,3584]{2,1,0:T(8,128)(2,1)} fusion(pred[1,256,3584]{2,1,0:T(32,128)(4,1)S(1)} %and_compare_fusion, bf16[256,3584]{1,0:T(8,128)(2,1)S(1)} %bitcast.34, bf16[1,256,3584]{2,1,0:T(8,128)(2,1)} %param.7, f32[3584]{0:T(1024)S(1)} %add_reduce_fusion, bf16[1,256,256]{2,1,0:T(8,128)(2,1)S(1)} %all-reduce.1), kind=kOutput, calls=%fused_computation.6 | convolution fusion | flops 475267072 | bytes 6567936 | tf_op jit(solution)/shard_map/ers,erf->esf/dot_general | solution.py:57
  (4 shorter events, 0.1 us)
Async XLA Ops:
  0.0 1.6 %copy-start = (bf16[16,3584]{1,0:T(8,128)(2,1)S(1)}, bf16[16,3584]{1,0:T(8,128)(2,1)}, u32[]{:S(2)}) copy-start(bf16[16,3584]{1,0:T(8,128)(2,1)} %param.5) | copy-start | bytes 344068
  0.0 9.7 %copy-start.1 = (s32[256,112]{0,1:T(8,128)S(1)}, s32[256,112]{0,1:T(8,128)}, u32[]{:S(2)}) copy-start(s32[256,112]{0,1:T(8,128)} %param.8) | copy-start | bytes 344068
  3.5 47.9 %all-to-all-start = ((bf16[1,16,1,16,3584]{4,3,2,0,1:T(8,128)(2,1)}), bf16[1,16,1,16,3584]{4,3,2,0,1:T(8,128)(2,1)S(1)}, u32[]{:S(2)}, u32[]{:S(2)}) async-start(bf16[1,16,1,16,3584]{4,3,2,0,1:T(8,128)(2,1)} %bitcast.35), calls=%async_computation | async-start | bytes 3670016 | tf_op jit(solution)/shard_map/all_to_all | solution.py:50
  19.8 46.5 %copy-start.2 = (f32[1,3584]{1,0:T(1,128)S(1)}, f32[1,3584]{1,0:T(1,128)}, u32[]{:S(2)}) copy-start(f32[1,3584]{1,0:T(1,128)} %param.9) | copy-start | bytes 43012
where the time goes:
time: 70.7 us; the launch traced here: 70.3 us
  waiting for transfers between devices  31.5 us (45%)
  blocking collectives  12.2 us (17%)
  local copies, waits for them, and re-layouts  8.32 us (12%)
  matrix products  8 us (11%)
  starting transfers between devices  6.24 us (9%)
  other arithmetic  3.88 us (5%)
    all_to_all x1, waiting for transfers between devices, local(): lax.all_to_all(packed, ('expert', 'hrow'), split_axis=1, concat_axis=2, t...  31.5 us
    psum x1, blocking collectives, local(): projected = lax.psum(partials, 'hcol').astype(jnp.bfloat16)  12.2 us
    shift_right_arithmetic x4, local copies, waits for them, and re-layouts, unpack_bits(): jnp.right_shift(bits[:, :, None], bit_shifts[None, None, :])  7.34 us
    all_to_all x1, starting transfers between devices, local(): lax.all_to_all(packed, ('expert', 'hrow'), split_axis=1, concat_axis=2, t...  6.24 us
    dot_general x1, matrix products, local(): jnp.einsum('ers,erf->esf', projected, routed, preferred_element_type=jnp....  3.9 us
    eq x1, other arithmetic, local(): keep_mask = keep_flags[None, :, :] == 1  2.75 us
    dot_general x1, matrix products, local(): jnp.einsum('esf,exgcf->exgcs', pruned, block, preferred_element_type=jnp....  2.19 us
    dot_general x1, matrix products, route_rows(): jnp.dot(selector, tokens, preferred_element_type=jnp.float32)  1.91 us
  transfers between devices with their start and end apart: 1, of which 1 were waited for; matrix products, arithmetic and copies ran while one was open for 14% of the time, Pallas kernels for 0%

commit v1 on v0

--- a/solution.py
+++ b/solution.py
@@ -1,6 +1,10 @@
+import functools
+
 import jax
 import jax.numpy as jnp
 from jax import lax
+from jax.experimental import pallas as pl
+from jax.experimental.pallas import tpu as pltpu
 from jax.sharding import PartitionSpec as P
 
 ROWS_E = 128
@@ -64,6 +68,246 @@
     return jnp.where(keep_mask, updated, jnp.float32(0.0)).astype(jnp.bfloat16)
 
 
+MESH = pl.DeviceIdType.MESH
+FLAGS = 128
+CHUNK = 256
+
+
+def kernel(tok_hbm, ids_hbm, w_hbm, bits_hbm, damp_hbm, out_hbm,
+           held, w_ref, pruned, keep, part, other, squares, ids_ref, bits_ref, words, damp_ref, out_ref,
+           load_sem, recv_sem, x_sem, core_sem, pair_sem, inner_sem, y_send, y_recv, store_sem):
+    z, cross, y = lax.axis_index("expert"), lax.axis_index("hrow"), lax.axis_index("hcol")
+    tok_count, feat = tok_hbm.shape
+    slab = w_hbm.shape[1]
+    half = feat // 256 * 128
+    spans = ((0, half), (half, feat + FLAGS - half))
+    x, core = cross // 2, cross % 2
+    upper = z // 2
+    inner = (z + 1) // 2 % 2
+    mate = 4 * upper + 1 - z
+    across = 3 - z
+    order = (z, mate, 2 - upper, 3 - 3 * upper)
+    x_row, core_row = (1 - x) * 2 + core, x * 2 + 1 - core
+    both_row = (1 - x) * 2 + 1 - core
+    to_mate, to_across = (mate, cross, y), (across, cross, y)
+    to_x, to_core, to_y = (z, x_row, y), (z, core_row, y), (z, cross, 1 - y)
+    mine = z * 4 + cross
+
+    loads = [
+        pltpu.make_async_copy(tok_hbm, held.at[mine, :, pl.ds(0, feat)], load_sem.at[0]),
+        pltpu.make_async_copy(ids_hbm, ids_ref, load_sem.at[1]),
+        pltpu.make_async_copy(bits_hbm, bits_ref, load_sem.at[2]),
+        pltpu.make_async_copy(w_hbm.at[0], w_ref, load_sem.at[3]),
+        pltpu.make_async_copy(damp_hbm, damp_ref, load_sem.at[4]),
+    ]
+    barrier = pltpu.get_barrier_semaphore()
+    for device in (to_mate, to_x, to_core, to_y):
+        pl.semaphore_signal(barrier, inc=1, device_id=device, device_id_type=MESH)
+
+    @pl.when(inner == 1)
+    def _():
+        pl.semaphore_signal(barrier, inc=1, device_id=to_across, device_id_type=MESH)
+
+    for load in loads:
+        load.start()
+
+    def block(number, h, sem, device):
+        lo, size = spans[h]
+        piece = held.at[number, :, pl.ds(lo, size)]
+        return pltpu.make_async_remote_copy(
+            src_ref=piece, dst_ref=piece, send_sem=sem, recv_sem=recv_sem.at[number, h],
+            device_id=device, device_id_type=MESH)
+
+    def arrived(number, h):
+        block(number, h, x_sem.at[0, 0], to_x).wait_recv()
+
+    always, inners = [], []
+
+    def send(number, h, sem, device):
+        copy = block(number, h, sem, device)
+        copy.start()
+        always.append(copy)
+
+    def forward(step, number, h):
+        if step == 0:
+            send(number, h, pair_sem.at[0, h], to_mate)
+        else:
+            where, sem = ((to_across, inner_sem.at[1, h]) if step == 1 else (to_mate, pair_sem.at[step, h]))
+
+            @pl.when(inner == 1)
+            def _():
+                block(number, h, sem, where).start()
+
+            inners.append(block(number, h, sem, where))
+        if step == 0:
+
+            @pl.when(inner == 1)
+            def _():
+                block(number, h, inner_sem.at[0, h], to_across).start()
+
+            inners.append(block(number, h, inner_sem.at[0, h], to_across))
+        if not (step == 1 and h == 1):
+            send(number, h, x_sem.at[step, h], to_x)
+        send(number, h, core_sem.at[step, h], to_core)
+
+    def crossed(step):
+        number = order[step] * 4 + x_row
+        for h in (0, 1):
+            arrived(number, h)
+            if step == 0 and h == 1:
+                send(number, h, pair_sem.at[1, 0], to_mate)
+            send(number, h, core_sem.at[4 + step, h], to_core)
+
+    def column(step):
+        number = order[step] * 4 + cross
+        for h in (0, 1):
+            arrived(number, h)
+            forward(step, number, h)
+
+    def plane_of(step):
+        rows = 4 * tok_count
+        return pl.ds(pl.multiple_of(order[step] * rows, rows), rows)
+
+    def y_copy(step):
+        rows = plane_of(step)
+        return pltpu.make_async_remote_copy(
+            src_ref=part.at[rows, :], dst_ref=other.at[rows, :], send_sem=y_send.at[step],
+            recv_sem=y_recv.at[step], device_id=to_y, device_id_type=MESH)
+
+    def member(flags):
+        lane = lax.broadcasted_iota(jnp.int32, flags.shape, 1)
+        return jnp.sum(jnp.where(lane == mine, flags.astype(jnp.float32), 0.0), axis=1, keepdims=True)
+
+    def project(step):
+        for h in (0, 1):
+            arrived(order[step] * 4 + core_row, h)
+            arrived(order[step] * 4 + both_row, h)
+        rows = plane_of(step)
+        blocks = pl.ds(order[step] * 4, 4)
+        tokens = held[blocks, :, 0:feat].reshape(4 * tok_count, feat)
+        part[rows, :] = lax.dot_general(
+            tokens, pruned[...], (((1,), (1,)), ((), ())), preferred_element_type=jnp.float32)
+        y_copy(step).start()
+        here = member(held[blocks, :, feat:feat + FLAGS].reshape(4 * tok_count, FLAGS))
+        for lo in range(0, feat, CHUNK):
+            piece = held[blocks, :, lo:lo + CHUNK].reshape(4 * tok_count, CHUNK).astype(jnp.float32)
+            total = jnp.sum((piece * piece * here).reshape(-1, 8, CHUNK), axis=0)
+            squares[:, lo:lo + CHUNK] = total if step == 0 else squares[:, lo:lo + CHUNK] + total
+
+    loads[1].wait()
+    ids = ids_ref[...]
+    lane = lax.broadcasted_iota(jnp.int32, (tok_count, FLAGS), 1)
+    named = jnp.zeros((tok_count, FLAGS), jnp.float32)
+    for k in range(ids.shape[1]):
+        named = jnp.where(ids[:, k:k + 1] == lane, 1.0, named)
+    held[mine, :, feat:feat + FLAGS] = named.astype(jnp.bfloat16)
+    loads[0].wait()
+    pl.semaphore_wait(barrier, 4 + inner)
+
+    for h in (0, 1):
+        forward(0, mine, h)
+
+    loads[2].wait()
+    loads[3].wait()
+    words[...] = jnp.zeros_like(words)
+    words[:, 0:bits_ref.shape[1]] = bits_ref[...]
+
+    def unpack(j, carry):
+        at = pl.ds(pl.multiple_of(j * 128, 128), 128)
+        spot = lax.broadcasted_iota(jnp.int32, (slab, 128), 1)
+        word = jnp.take_along_axis(words[...], 4 * j + spot // 32, axis=1)
+        bit = jnp.bitwise_and(jnp.right_shift(word, spot % 32), 1)
+        flag = bit.astype(jnp.float32)
+        keep[:, at] = flag.astype(jnp.bfloat16)
+        pruned[:, at] = jnp.where(bit == 1, 0.0, w_ref[:, at].astype(jnp.float32)).astype(jnp.bfloat16)
+        return carry
+
+    lax.fori_loop(0, feat // 128, unpack, 0)
+    loads[4].wait()
+
+    column(1)
+    crossed(0)
+    project(0)
+    column(2)
+    crossed(1)
+    project(1)
+    column(3)
+    crossed(2)
+    project(2)
+    crossed(3)
+    project(3)
+
+    here = member(held[:, :, feat:feat + FLAGS].reshape(-1, FLAGS))
+    for step in range(4):
+        y_copy(step).wait_recv()
+    projected = jnp.where(here > 0.5, part[...] + other[...], 0.0).T.astype(jnp.bfloat16)
+    stores = []
+    for lo in range(0, feat, CHUNK):
+        at = slice(lo, lo + CHUNK)
+        routed = held[:, :, at].reshape(-1, CHUNK)
+        comp = jnp.dot(projected, routed, preferred_element_type=jnp.float32)
+        diag = jnp.sum(squares[:, at], axis=0, keepdims=True) / ROWS_E + damp_ref[:, at]
+        updated = w_ref[:, at].astype(jnp.float32) + comp * (ETA / ROWS_E / diag)
+        out_ref[:, at] = updated.astype(jnp.bfloat16) * keep[:, at]
+        store = pltpu.make_async_copy(out_ref.at[:, at], out_hbm.at[0, :, at], store_sem.at[lo // CHUNK])
+        store.start()
+        stores.append(store)
+
+    for copy in always:
+        copy.wait_send()
+    for step in range(4):
+        y_copy(step).wait_send()
+
+    @pl.when(inner == 1)
+    def _():
+        for copy in inners:
+            copy.wait_send()
+
+    for store in stores:
+        store.wait()
+
+
+def gathered(tokens, expert_ids, weight, mask_bits, damping):
+    tok_count, feat = tokens.shape
+    slab = weight.shape[1]
+    blocks = 16
+    total = blocks * tok_count
+    dma = pltpu.SemaphoreType.DMA
+    return pl.pallas_call(
+        kernel,
+        out_shape=jax.ShapeDtypeStruct(weight.shape, jnp.bfloat16),
+        in_specs=[pl.BlockSpec(memory_space=pl.ANY)] * 5,
+        out_specs=pl.BlockSpec(memory_space=pl.ANY),
+        scratch_shapes=[
+            pltpu.VMEM((blocks, tok_count, feat + FLAGS), jnp.bfloat16),
+            pltpu.VMEM((slab, feat), jnp.bfloat16),
+            pltpu.VMEM((slab, feat), jnp.bfloat16),
+            pltpu.VMEM((slab, feat), jnp.bfloat16),
+            pltpu.VMEM((total, slab), jnp.float32),
+            pltpu.VMEM((total, slab), jnp.float32),
+            pltpu.VMEM((8, feat), jnp.float32),
+            pltpu.VMEM(expert_ids.shape, jnp.int32),
+            pltpu.VMEM(mask_bits.shape, jnp.int32),
+            pltpu.VMEM((slab, 128), jnp.int32),
+            pltpu.VMEM((1, feat), jnp.float32),
+            pltpu.VMEM((slab, feat), jnp.bfloat16),
+            dma((5,)),
+            dma((blocks, 2)),
+            dma((4, 2)),
+            dma((8, 2)),
+            dma((4, 2)),
+            dma((2, 2)),
+            dma((4,)),
+            dma((4,)),
+            dma((feat // CHUNK,)),
+        ],
+        compiler_params=pltpu.CompilerParams(
+            collective_id=0, has_side_effects=True, vmem_limit_bytes=40 * 1024 * 1024),
+        cost_estimate=pl.CostEstimate(
+            flops=4 * total * slab * feat, bytes_accessed=4 * slab * feat, transcendentals=0),
+    )(tokens, expert_ids, weight, mask_bits, damping)
+
+
 def solution(mesh):
     in_specs = (
         P(("expert", "hrow"), "hcol"),
@@ -73,4 +317,14 @@
         P(("expert", "hrow"), "hcol"),
     )
     out_specs = P(("expert", "hrow"), None, "hcol")
-    return jax.shard_map(local, mesh=mesh, in_specs=in_specs, out_specs=out_specs, check_vma=False)
+    line, cross = mesh.shape["expert"], mesh.shape["hrow"]
+
+    def body(tokens, expert_ids, weight, mask_bits, damping):
+        tok_count, top_count = expert_ids.shape
+        capacity = 2 * tok_count * top_count // (line * cross * weight.shape[0])
+        fits = line == 4 and cross == 4 and mesh.shape["hcol"] == 2 and weight.shape[0] == 1
+        if fits and capacity >= tok_count:
+            return gathered(tokens, expert_ids, weight, mask_bits, damping)
+        return local(tokens, expert_ids, weight, mask_bits, damping)
+
+    return jax.shard_map(body, mesh=mesh, in_specs=in_specs, out_specs=out_specs, check_vma=False)

time: 70.7 us -> 37.7 us (0.53)
  the two profiles are of different devices: /device:TPU:10 before, /device:TPU:0 now
where the time goes in v1:
time: 37.7 us; the launch traced here: 37.4 us
  Pallas kernels  31.3 us (83%)
  local copies, waits for them, and re-layouts  6.08 us (16%)
    pallas_call x1, Pallas kernels, gathered(): pl.pallas_call(kernel, out_shape=jax.ShapeDtypeStruct(weight.shape, jnp.b...  31.3 us
    unnamed x9, local copies, waits for them, and re-layouts  6.08 us

profile of v1, /device:TPU:0, one launch (start us, length us, event | category | flops | bytes accessed | tf_op | source)
XLA Modules:
  0.0 37.4 jit_solution(5672165684067727438)
XLA Ops:
  0.0 0.8 %copy.6.ids_hbm = s32[16,8]{1,0:T(8,128)S(1)} copy(s32[16,8]{0,1:T(8,128)} %param.6) | data formatting | bytes 1024 | tf_op args[1]
  0.8 1.0 %copy.7.bits_hbm = s32[256,112]{1,0:T(8,128)S(1)} copy(s32[256,112]{0,1:T(8,128)} %param.8) | data formatting | bytes 229376 | tf_op args[3]
  1.8 0.0 copy-start
  1.8 1.5 %copy-done = bf16[1,256,3584]{2,1,0:T(8,128)(2,1)S(1)} copy-done((bf16[1,256,3584]{2,1,0:T(8,128)(2,1)S(1)}, bf16[1,256,3584]{2,1,0:T(8,128)(2,1)}, u32[]{:S(2)}) %copy-start) | copy-done | bytes 1835032
  3.3 0.0 copy-start.1
  3.3 0.9 %copy-done.1 = bf16[16,3584]{1,0:T(8,128)(2,1)S(1)} copy-done((bf16[16,3584]{1,0:T(8,128)(2,1)S(1)}, bf16[16,3584]{1,0:T(8,128)(2,1)}, u32[]{:S(2)}) %copy-start.1) | copy-done | bytes 114712
  4.2 0.0 copy-start.2
  4.2 0.7 %copy-done.2 = f32[1,3584]{1,0:T(1,128)S(1)} copy-done((f32[1,3584]{1,0:T(1,128)S(1)}, f32[1,3584]{1,0:T(1,128)}, u32[]{:S(2)}) %copy-start.2) | copy-done | bytes 14360
  4.9 31.3 %shard_map.55 = bf16[1,256,3584]{2,1,0:T(8,128)(2,1)S(1)} custom-call(bf16[16,3584]{1,0:T(8,128)(2,1)S(1)} %copy-done.1, s32[16,8]{1,0:T(8,128)S(1)} %copy.6.ids_hbm, bf16[1,256,3584]{2,1,0:T(8,128)(2,1)S(1)} %copy-done, s32[256,112]{1,0:T(8,128)S(1)} %copy.7.bits_hbm, f32[1,3584]{1,0:T(1,128)S(1)} %copy-done.2), custom_call_target="tpu_custom_call" | custom-call | flops 939524096 | bytes 3670016 | tf_op jit(solution)/shard_map/pallas_call | solution.py:276
  36.2 1.2 %copy.9 = bf16[1,256,3584]{2,1,0:T(8,128)(2,1)} copy(bf16[1,256,3584]{2,1,0:T(8,128)(2,1)S(1)} %shard_map.55) | data formatting | bytes 3670016
Async XLA Ops:
  1.8 1.5 %copy-start = (bf16[1,256,3584]{2,1,0:T(8,128)(2,1)S(1)}, bf16[1,256,3584]{2,1,0:T(8,128)(2,1)}, u32[]{:S(2)}) copy-start(bf16[1,256,3584]{2,1,0:T(8,128)(2,1)} %w_hbm.1) | copy-start | bytes 5505028
  3.3 0.9 %copy-start.1 = (bf16[16,3584]{1,0:T(8,128)(2,1)S(1)}, bf16[16,3584]{1,0:T(8,128)(2,1)}, u32[]{:S(2)}) copy-start(bf16[16,3584]{1,0:T(8,128)(2,1)} %tok_hbm.1) | copy-start | bytes 344068
  4.2 0.7 %copy-start.2 = (f32[1,3584]{1,0:T(1,128)S(1)}, f32[1,3584]{1,0:T(1,128)}, u32[]{:S(2)}) copy-start(f32[1,3584]{1,0:T(1,128)} %damp_hbm.1) | copy-start | bytes 43012

commit v2 on v1

--- a/solution.py
+++ b/solution.py
@@ -74,8 +74,8 @@
 
 
 def kernel(tok_hbm, ids_hbm, w_hbm, bits_hbm, damp_hbm, out_hbm,
-           held, w_ref, pruned, keep, part, other, squares, ids_ref, bits_ref, words, damp_ref, out_ref,
-           load_sem, recv_sem, x_sem, core_sem, pair_sem, inner_sem, y_send, y_recv, store_sem):
+           held, w_ref, pruned, keep, part, other, squares, ids_ref, wide_ids, bits_ref, words, damp_ref, out_ref,
+           load_sem, recv_sem, x_sem, core_sem, mate_sem, far_sem, across_sem, y_send, y_recv, store_sem):
     z, cross, y = lax.axis_index("expert"), lax.axis_index("hrow"), lax.axis_index("hcol")
     tok_count, feat = tok_hbm.shape
     slab = w_hbm.shape[1]
@@ -86,22 +86,25 @@
     inner = (z + 1) // 2 % 2
     mate = 4 * upper + 1 - z
     across = 3 - z
+    far = (z + 2) % 4
     order = (z, mate, 2 - upper, 3 - 3 * upper)
     x_row, core_row = (1 - x) * 2 + core, x * 2 + 1 - core
     both_row = (1 - x) * 2 + 1 - core
-    to_mate, to_across = (mate, cross, y), (across, cross, y)
+    to_mate, to_across, to_far = (mate, cross, y), (across, cross, y), (far, cross, y)
+    to_first = (mate * inner + far * (1 - inner), cross, y)
+    to_second = (far * inner + mate * (1 - inner), cross, y)
     to_x, to_core, to_y = (z, x_row, y), (z, core_row, y), (z, cross, 1 - y)
     mine = z * 4 + cross
 
     loads = [
         pltpu.make_async_copy(tok_hbm, held.at[mine, :, pl.ds(0, feat)], load_sem.at[0]),
         pltpu.make_async_copy(ids_hbm, ids_ref, load_sem.at[1]),
-        pltpu.make_async_copy(bits_hbm, bits_ref, load_sem.at[2]),
+        pltpu.make_async_copy(bits_hbm, bits_ref.at[pl.ds(0, bits_hbm.shape[0]), :], load_sem.at[2]),
         pltpu.make_async_copy(w_hbm.at[0], w_ref, load_sem.at[3]),
         pltpu.make_async_copy(damp_hbm, damp_ref, load_sem.at[4]),
     ]
     barrier = pltpu.get_barrier_semaphore()
-    for device in (to_mate, to_x, to_core, to_y):
+    for device in (to_mate, to_far, to_x, to_core, to_y):
         pl.semaphore_signal(barrier, inc=1, device_id=device, device_id_type=MESH)
 
     @pl.when(inner == 1)
@@ -128,89 +131,99 @@
         copy.start()
         always.append(copy)
 
-    def forward(step, number, h):
-        if step == 0:
-            send(number, h, pair_sem.at[0, h], to_mate)
-        else:
-            where, sem = ((to_across, inner_sem.at[1, h]) if step == 1 else (to_mate, pair_sem.at[step, h]))
-
-            @pl.when(inner == 1)
-            def _():
-                block(number, h, sem, where).start()
-
-            inners.append(block(number, h, sem, where))
-        if step == 0:
-
-            @pl.when(inner == 1)
-            def _():
-                block(number, h, inner_sem.at[0, h], to_across).start()
-
-            inners.append(block(number, h, inner_sem.at[0, h], to_across))
-        if not (step == 1 and h == 1):
-            send(number, h, x_sem.at[step, h], to_x)
-        send(number, h, core_sem.at[step, h], to_core)
+    def spread(number, h):
+        send(number, h, x_sem.at[0, h], to_x)
+
+        @pl.when(inner == 1)
+        def _():
+            block(number, h, across_sem.at[h], to_across).start()
+
+        inners.append(block(number, h, across_sem.at[h], to_across))
+        send(number, h, mate_sem.at[0, h], to_first)
+        send(number, h, far_sem.at[h], to_second)
+        send(number, h, core_sem.at[0, h], to_core)
+
+    def column(step):
+        number = order[step] * 4 + cross
+        for h in (0, 1):
+            arrived(number, h)
+            if step == 3:
+
+                @pl.when(inner == 1)
+                def _():
+                    block(number, h, mate_sem.at[2, h], to_mate).start()
+
+                inners.append(block(number, h, mate_sem.at[2, h], to_mate))
+            if not (step == 1 and h == 1):
+                send(number, h, x_sem.at[step, h], to_x)
+            send(number, h, core_sem.at[step, h], to_core)
 
     def crossed(step):
         number = order[step] * 4 + x_row
         for h in (0, 1):
             arrived(number, h)
             if step == 0 and h == 1:
-                send(number, h, pair_sem.at[1, 0], to_mate)
+                send(number, h, mate_sem.at[1, 0], to_mate)
             send(number, h, core_sem.at[4 + step, h], to_core)
 
-    def column(step):
-        number = order[step] * 4 + cross
-        for h in (0, 1):
-            arrived(number, h)
-            forward(step, number, h)
-
-    def plane_of(step):
-        rows = 4 * tok_count
-        return pl.ds(pl.multiple_of(order[step] * rows, rows), rows)
-
-    def y_copy(step):
-        rows = plane_of(step)
+    def rows_of(first, count):
+        return pl.ds(pl.multiple_of(first * tok_count, tok_count), count * tok_count)
+
+    def y_copy(first, count, which):
+        rows = rows_of(first, count)
         return pltpu.make_async_remote_copy(
-            src_ref=part.at[rows, :], dst_ref=other.at[rows, :], send_sem=y_send.at[step],
-            recv_sem=y_recv.at[step], device_id=to_y, device_id_type=MESH)
+            src_ref=part.at[rows, :], dst_ref=other.at[rows, :], send_sem=y_send.at[which],
+            recv_sem=y_recv.at[which], device_id=to_y, device_id_type=MESH)
 
     def member(flags):
         lane = lax.broadcasted_iota(jnp.int32, flags.shape, 1)
         return jnp.sum(jnp.where(lane == mine, flags.astype(jnp.float32), 0.0), axis=1, keepdims=True)
 
-    def project(step):
+    summed = []
+
+    def project(first, count):
+        rows, blocks = count * tok_count, pl.ds(first, count)
+        tokens = held[blocks, :, 0:feat].reshape(rows, feat)
+        part[rows_of(first, count), :] = lax.dot_general(
+            tokens, pruned[...], (((1,), (1,)), ((), ())), preferred_element_type=jnp.float32)
+        copy = y_copy(first, count, len(summed))
+        copy.start()
+        summed.append(copy)
+        here = member(held[blocks, :, feat:feat + FLAGS].reshape(rows, FLAGS))
+        for lo in range(0, feat, CHUNK):
+            piece = held[blocks, :, lo:lo + CHUNK].reshape(rows, CHUNK).astype(jnp.float32)
+            total = jnp.sum((piece * piece * here).reshape(-1, 8, CHUNK), axis=0)
+            squares[:, lo:lo + CHUNK] = total if len(summed) == 1 else squares[:, lo:lo + CHUNK] + total
+
+    def other_core(step, row):
         for h in (0, 1):
-            arrived(order[step] * 4 + core_row, h)
-            arrived(order[step] * 4 + both_row, h)
-        rows = plane_of(step)
-        blocks = pl.ds(order[step] * 4, 4)
-        tokens = held[blocks, :, 0:feat].reshape(4 * tok_count, feat)
-        part[rows, :] = lax.dot_general(
-            tokens, pruned[...], (((1,), (1,)), ((), ())), preferred_element_type=jnp.float32)
-        y_copy(step).start()
-        here = member(held[blocks, :, feat:feat + FLAGS].reshape(4 * tok_count, FLAGS))
-        for lo in range(0, feat, CHUNK):
-            piece = held[blocks, :, lo:lo + CHUNK].reshape(4 * tok_count, CHUNK).astype(jnp.float32)
-            total = jnp.sum((piece * piece * here).reshape(-1, 8, CHUNK), axis=0)
-            squares[:, lo:lo + CHUNK] = total if step == 0 else squares[:, lo:lo + CHUNK] + total
+            arrived(order[step] * 4 + row, h)
+
+    def plane(step):
+        other_core(step, core_row)
+        other_core(step, both_row)
+        project(order[step] * 4, 4)
 
     loads[1].wait()
-    ids = ids_ref[...]
-    lane = lax.broadcasted_iota(jnp.int32, (tok_count, FLAGS), 1)
-    named = jnp.zeros((tok_count, FLAGS), jnp.float32)
-    for k in range(ids.shape[1]):
-        named = jnp.where(ids[:, k:k + 1] == lane, 1.0, named)
-    held[mine, :, feat:feat + FLAGS] = named.astype(jnp.bfloat16)
+    wide_ids[...] = jnp.full_like(wide_ids, -1)
+    wide_ids[:, 0:tok_count] = ids_ref[...]
+    expert = lax.broadcasted_iota(jnp.int32, (FLAGS, 128), 0)
+    named = jnp.zeros((FLAGS, 128), jnp.float32)
+    for k in range(ids_ref.shape[0]):
+        named = jnp.where(wide_ids[k:k + 1, :] == expert, 1.0, named)
+    held[mine, :, feat:feat + FLAGS] = named.T[0:tok_count, :].astype(jnp.bfloat16)
     loads[0].wait()
-    pl.semaphore_wait(barrier, 4 + inner)
+    pl.semaphore_wait(barrier, 5 + inner)
 
     for h in (0, 1):
-        forward(0, mine, h)
-
+        spread(mine, h)
+
+    filled = bits_hbm.shape[0]
+    if filled < 128:
+        bits_ref[filled:128, :] = jnp.zeros((128 - filled, slab), jnp.int32)
     loads[2].wait()
     loads[3].wait()
-    words[...] = jnp.zeros_like(words)
-    words[:, 0:bits_ref.shape[1]] = bits_ref[...]
+    words[...] = bits_ref[...].T
 
     def unpack(j, carry):
         at = pl.ds(pl.multiple_of(j * 128, 128), 128)
@@ -222,24 +235,28 @@
         pruned[:, at] = jnp.where(bit == 1, 0.0, w_ref[:, at].astype(jnp.float32)).astype(jnp.bfloat16)
         return carry
 
-    lax.fori_loop(0, feat // 128, unpack, 0)
-    loads[4].wait()
-
+    steps = feat // 128
+    lax.fori_loop(0, steps // 2, unpack, 0)
     column(1)
     crossed(0)
-    project(0)
+    lax.fori_loop(steps // 2, steps, unpack, 0)
     column(2)
     crossed(1)
-    project(1)
+    plane(0)
+    plane(1)
     column(3)
     crossed(2)
-    project(2)
+    plane(2)
+    other_core(3, core_row)
+    project(order[3] * 4 + 2 * x, 2)
     crossed(3)
-    project(3)
-
+    other_core(3, both_row)
+    project(order[3] * 4 + 2 * (1 - x), 2)
+
+    loads[4].wait()
     here = member(held[:, :, feat:feat + FLAGS].reshape(-1, FLAGS))
-    for step in range(4):
-        y_copy(step).wait_recv()
+    for copy in summed:
+        copy.wait_recv()
     projected = jnp.where(here > 0.5, part[...] + other[...], 0.0).T.astype(jnp.bfloat16)
     stores = []
     for lo in range(0, feat, CHUNK):
@@ -255,8 +272,8 @@
 
     for copy in always:
         copy.wait_send()
-    for step in range(4):
-        y_copy(step).wait_send()
+    for copy in summed:
+        copy.wait_send()
 
     @pl.when(inner == 1)
     def _():
@@ -276,7 +293,7 @@
     return pl.pallas_call(
         kernel,
         out_shape=jax.ShapeDtypeStruct(weight.shape, jnp.bfloat16),
-        in_specs=[pl.BlockSpec(memory_space=pl.ANY)] * 5,
+        in_specs=[pl.BlockSpec(memory_space=pltpu.HBM)] * 5,
         out_specs=pl.BlockSpec(memory_space=pl.ANY),
         scratch_shapes=[
             pltpu.VMEM((blocks, tok_count, feat + FLAGS), jnp.bfloat16),
@@ -286,8 +303,9 @@
             pltpu.VMEM((total, slab), jnp.float32),
             pltpu.VMEM((total, slab), jnp.float32),
             pltpu.VMEM((8, feat), jnp.float32),
-            pltpu.VMEM(expert_ids.shape, jnp.int32),
-            pltpu.VMEM(mask_bits.shape, jnp.int32),
+            pltpu.VMEM((expert_ids.shape[1], tok_count), jnp.int32),
+            pltpu.VMEM((expert_ids.shape[1], 128), jnp.int32),
+            pltpu.VMEM((128, slab), jnp.int32),
             pltpu.VMEM((slab, 128), jnp.int32),
             pltpu.VMEM((1, feat), jnp.float32),
             pltpu.VMEM((slab, feat), jnp.bfloat16),
@@ -295,17 +313,18 @@
             dma((blocks, 2)),
             dma((4, 2)),
             dma((8, 2)),
-            dma((4, 2)),
-            dma((2, 2)),
-            dma((4,)),
-            dma((4,)),
+            dma((3, 2)),
+            dma((2,)),
+            dma((2,)),
+            dma((5,)),
+            dma((5,)),
             dma((feat // CHUNK,)),
         ],
         compiler_params=pltpu.CompilerParams(
-            collective_id=0, has_side_effects=True, vmem_limit_bytes=40 * 1024 * 1024),
+            collective_id=0, has_side_effects=True, vmem_limit_bytes=63 * 1024 * 1024),
         cost_estimate=pl.CostEstimate(
             flops=4 * total * slab * feat, bytes_accessed=4 * slab * feat, transcendentals=0),
-    )(tokens, expert_ids, weight, mask_bits, damping)
+    )(tokens, expert_ids.T, weight, mask_bits.T, damping)
 
 
 def solution(mesh):

time: 37.7 us -> 34.7 us (0.920)
  local copies, waits for them, and re-layouts: 6.08 us -> 2.85 us
  Pallas kernels: 31.3 us -> 31.7 us
    unnamed x9 -> x1, local copies, waits for them, and re-layouts: 6.08 us -> 2.85 us
where the time goes in v2:
time: 34.7 us; the launch traced here: 34.5 us
  Pallas kernels  31.7 us (91%)
  local copies, waits for them, and re-layouts  2.85 us (8%)
    pallas_call x1, Pallas kernels, gathered(): pl.pallas_call(kernel, out_shape=jax.ShapeDtypeStruct(weight.shape, jnp.b...  31.7 us
    unnamed x1, local copies, waits for them, and re-layouts  2.85 us

profile of v2, /device:TPU:0, one launch (start us, length us, event | category | flops | bytes accessed | tf_op | source)
XLA Modules:
  0.0 34.5 jit_solution(1335383554137532024)
XLA Ops:
  0.0 31.7 %shard_map.55 = bf16[1,256,3584]{2,1,0:T(8,128)(2,1)} custom-call(bf16[16,3584]{1,0:T(8,128)(2,1)} %tok_hbm.1, s32[8,16]{1,0:T(8,128)} %bitcast.3, bf16[1,256,3584]{2,1,0:T(8,128)(2,1)} %w_hbm.1, s32[112,256]{1,0:T(8,128)} %bitcast.2, f32[1,3584]{1,0:T(1,128)} %damp_hbm.1), custom_call_target="tpu_custom_call" | custom-call | flops 939524096 | bytes 3670016 | tf_op jit(solution)/shard_map/pallas_call | solution.py:293
  31.7 2.8 %copy.7 = bf16[1,256,3584]{2,1,0:T(8,128)(2,1)} copy(bf16[1,256,3584]{2,1,0:T(8,128)(2,1)} %shard_map.55) | data formatting | bytes 3670016

commit v3 on v2

--- a/solution.py
+++ b/solution.py
@@ -71,6 +71,7 @@
 MESH = pl.DeviceIdType.MESH
 FLAGS = 128
 CHUNK = 256
+WIDE = 512
 
 
 def kernel(tok_hbm, ids_hbm, w_hbm, bits_hbm, damp_hbm, out_hbm,
@@ -185,7 +186,7 @@
         rows, blocks = count * tok_count, pl.ds(first, count)
         tokens = held[blocks, :, 0:feat].reshape(rows, feat)
         part[rows_of(first, count), :] = lax.dot_general(
-            tokens, pruned[...], (((1,), (1,)), ((), ())), preferred_element_type=jnp.float32)
+            pruned[...], tokens, (((1,), (1,)), ((), ())), preferred_element_type=jnp.float32).T
         copy = y_copy(first, count, len(summed))
         copy.start()
         summed.append(copy)
@@ -225,14 +226,17 @@
     loads[3].wait()
     words[...] = bits_ref[...].T
 
+    spot = lax.broadcasted_iota(jnp.int32, (1, 128), 1)
+    group = jnp.right_shift(spot, 5)
+    probe = jnp.left_shift(jnp.int32(1), jnp.bitwise_and(spot, 31))
+
     def unpack(j, carry):
         at = pl.ds(pl.multiple_of(j * 128, 128), 128)
-        spot = lax.broadcasted_iota(jnp.int32, (slab, 128), 1)
-        word = jnp.take_along_axis(words[...], 4 * j + spot // 32, axis=1)
-        bit = jnp.bitwise_and(jnp.right_shift(word, spot % 32), 1)
-        flag = bit.astype(jnp.float32)
-        keep[:, at] = flag.astype(jnp.bfloat16)
-        pruned[:, at] = jnp.where(bit == 1, 0.0, w_ref[:, at].astype(jnp.float32)).astype(jnp.bfloat16)
+        index = jnp.broadcast_to(group + 4 * j, (slab, 128))
+        word = jnp.take_along_axis(words[...], index, axis=1)
+        flag = jnp.where(jnp.bitwise_and(word, probe) != 0, 1.0, 0.0).astype(jnp.bfloat16)
+        keep[:, at] = flag
+        pruned[:, at] = w_ref[:, at] * (jnp.bfloat16(1.0) - flag)
         return carry
 
     steps = feat // 128
@@ -259,14 +263,14 @@
         copy.wait_recv()
     projected = jnp.where(here > 0.5, part[...] + other[...], 0.0).T.astype(jnp.bfloat16)
     stores = []
-    for lo in range(0, feat, CHUNK):
-        at = slice(lo, lo + CHUNK)
-        routed = held[:, :, at].reshape(-1, CHUNK)
+    for lo in range(0, feat, WIDE):
+        at = slice(lo, lo + WIDE)
+        routed = held[:, :, at].reshape(-1, WIDE)
         comp = jnp.dot(projected, routed, preferred_element_type=jnp.float32)
         diag = jnp.sum(squares[:, at], axis=0, keepdims=True) / ROWS_E + damp_ref[:, at]
         updated = w_ref[:, at].astype(jnp.float32) + comp * (ETA / ROWS_E / diag)
         out_ref[:, at] = updated.astype(jnp.bfloat16) * keep[:, at]
-        store = pltpu.make_async_copy(out_ref.at[:, at], out_hbm.at[0, :, at], store_sem.at[lo // CHUNK])
+        store = pltpu.make_async_copy(out_ref.at[:, at], out_hbm.at[0, :, at], store_sem.at[lo // WIDE])
         store.start()
         stores.append(store)
 
@@ -318,10 +322,10 @@
             dma((2,)),
             dma((5,)),
             dma((5,)),
-            dma((feat // CHUNK,)),
+            dma((feat // WIDE,)),
         ],
         compiler_params=pltpu.CompilerParams(
-            collective_id=0, has_side_effects=True, vmem_limit_bytes=63 * 1024 * 1024),
+            collective_id=0, has_side_effects=True, vmem_limit_bytes=62 * 1024 * 1024),
         cost_estimate=pl.CostEstimate(
             flops=4 * total * slab * feat, bytes_accessed=4 * slab * feat, transcendentals=0),
     )(tokens, expert_ids.T, weight, mask_bits.T, damping)

time: 34.7 us -> 35 us (level)
  no operation moved by 1% of the time
where the time goes in v3:
time: 35 us; the launch traced here: 34.8 us
  Pallas kernels  32 us (91%)
  local copies, waits for them, and re-layouts  2.85 us (8%)
    pallas_call x1, Pallas kernels, gathered(): pl.pallas_call(kernel, out_shape=jax.ShapeDtypeStruct(weight.shape, jnp.b...  32 us
    unnamed x1, local copies, waits for them, and re-layouts  2.85 us

profile of v3, /device:TPU:0, one launch (start us, length us, event | category | flops | bytes accessed | tf_op | source)
XLA Modules:
  0.0 34.8 jit_solution(7277115145852706829)
XLA Ops:
  0.0 32.0 %shard_map.55 = bf16[1,256,3584]{2,1,0:T(8,128)(2,1)} custom-call(bf16[16,3584]{1,0:T(8,128)(2,1)} %tok_hbm.1, s32[8,16]{1,0:T(8,128)} %bitcast.3, bf16[1,256,3584]{2,1,0:T(8,128)(2,1)} %w_hbm.1, s32[112,256]{1,0:T(8,128)} %bitcast.2, f32[1,3584]{1,0:T(1,128)} %damp_hbm.1), custom_call_target="tpu_custom_call" | custom-call | flops 939524096 | bytes 3670016 | tf_op jit(solution)/shard_map/pallas_call | solution.py:297
  32.0 2.8 %copy.7 = bf16[1,256,3584]{2,1,0:T(8,128)(2,1)} copy(bf16[1,256,3584]{2,1,0:T(8,128)(2,1)} %shard_map.55) | data formatting | bytes 3670016

commit v4 on v3

--- a/solution.py
+++ b/solution.py
@@ -76,7 +76,7 @@
 
 def kernel(tok_hbm, ids_hbm, w_hbm, bits_hbm, damp_hbm, out_hbm,
            held, w_ref, pruned, keep, part, other, squares, ids_ref, wide_ids, bits_ref, words, damp_ref, out_ref,
-           load_sem, recv_sem, x_sem, core_sem, mate_sem, far_sem, across_sem, y_send, y_recv, store_sem):
+           load_sem, recv_sem, x_sem, core_sem, line_sem, y_send, y_recv, store_sem):
     z, cross, y = lax.axis_index("expert"), lax.axis_index("hrow"), lax.axis_index("hcol")
     tok_count, feat = tok_hbm.shape
     slab = w_hbm.shape[1]
@@ -84,16 +84,12 @@
     spans = ((0, half), (half, feat + FLAGS - half))
     x, core = cross // 2, cross % 2
     upper = z // 2
-    inner = (z + 1) // 2 % 2
     mate = 4 * upper + 1 - z
-    across = 3 - z
-    far = (z + 2) % 4
     order = (z, mate, 2 - upper, 3 - 3 * upper)
     x_row, core_row = (1 - x) * 2 + core, x * 2 + 1 - core
     both_row = (1 - x) * 2 + 1 - core
-    to_mate, to_across, to_far = (mate, cross, y), (across, cross, y), (far, cross, y)
-    to_first = (mate * inner + far * (1 - inner), cross, y)
-    to_second = (far * inner + mate * (1 - inner), cross, y)
+    to_mate = (mate, cross, y)
+    to_line = [(order[step], cross, y) for step in (3, 2, 1)]
     to_x, to_core, to_y = (z, x_row, y), (z, core_row, y), (z, cross, 1 - y)
     mine = z * 4 + cross
 
@@ -105,12 +101,8 @@
         pltpu.make_async_copy(damp_hbm, damp_ref, load_sem.at[4]),
     ]
     barrier = pltpu.get_barrier_semaphore()
-    for device in (to_mate, to_far, to_x, to_core, to_y):
+    for device in to_line + [to_x, to_core, to_y]:
         pl.semaphore_signal(barrier, inc=1, device_id=device, device_id_type=MESH)
-
-    @pl.when(inner == 1)
-    def _():
-        pl.semaphore_signal(barrier, inc=1, device_id=to_across, device_id_type=MESH)
 
     for load in loads:
         load.start()
@@ -125,7 +117,7 @@
     def arrived(number, h):
         block(number, h, x_sem.at[0, 0], to_x).wait_recv()
 
-    always, inners = [], []
+    always = []
 
     def send(number, h, sem, device):
         copy = block(number, h, sem, device)
@@ -134,27 +126,14 @@
 
     def spread(number, h):
         send(number, h, x_sem.at[0, h], to_x)
-
-        @pl.when(inner == 1)
-        def _():
-            block(number, h, across_sem.at[h], to_across).start()
-
-        inners.append(block(number, h, across_sem.at[h], to_across))
-        send(number, h, mate_sem.at[0, h], to_first)
-        send(number, h, far_sem.at[h], to_second)
+        for place, device in enumerate(to_line):
+            send(number, h, line_sem.at[place, h], device)
         send(number, h, core_sem.at[0, h], to_core)
 
     def column(step):
         number = order[step] * 4 + cross
         for h in (0, 1):
             arrived(number, h)
-            if step == 3:
-
-                @pl.when(inner == 1)
-                def _():
-                    block(number, h, mate_sem.at[2, h], to_mate).start()
-
-                inners.append(block(number, h, mate_sem.at[2, h], to_mate))
             if not (step == 1 and h == 1):
                 send(number, h, x_sem.at[step, h], to_x)
             send(number, h, core_sem.at[step, h], to_core)
@@ -164,7 +143,7 @@
         for h in (0, 1):
             arrived(number, h)
             if step == 0 and h == 1:
-                send(number, h, mate_sem.at[1, 0], to_mate)
+                send(number, h, line_sem.at[3, 0], to_mate)
             send(number, h, core_sem.at[4 + step, h], to_core)
 
     def rows_of(first, count):
@@ -214,7 +193,7 @@
         named = jnp.where(wide_ids[k:k + 1, :] == expert, 1.0, named)
     held[mine, :, feat:feat + FLAGS] = named.T[0:tok_count, :].astype(jnp.bfloat16)
     loads[0].wait()
-    pl.semaphore_wait(barrier, 5 + inner)
+    pl.semaphore_wait(barrier, 6)
 
     for h in (0, 1):
         spread(mine, h)
@@ -278,11 +257,6 @@
         copy.wait_send()
     for copy in summed:
         copy.wait_send()
-
-    @pl.when(inner == 1)
-    def _():
-        for copy in inners:
-            copy.wait_send()
 
     for store in stores:
         store.wait()
@@ -317,9 +291,7 @@
             dma((blocks, 2)),
             dma((4, 2)),
             dma((8, 2)),
-            dma((3, 2)),
-            dma((2,)),
-            dma((2,)),
+            dma((4, 2)),
             dma((5,)),
             dma((5,)),
             dma((feat // WIDE,)),

time: 35 us -> 35.8 us (1.023)
  Pallas kernels: 32 us -> 32.8 us
    pallas_call x1, Pallas kernels: 32 us -> 32.8 us  [gathered(): pl.pallas_call(kernel, out_shape=jax.ShapeDtypeStruct(weight.shape, jnp.b...]
where the time goes in v4:
time: 35.8 us; the launch traced here: 35.7 us
  Pallas kernels  32.8 us (92%)
  local copies, waits for them, and re-layouts  2.85 us (8%)
    pallas_call x1, Pallas kernels, gathered(): pl.pallas_call(kernel, out_shape=jax.ShapeDtypeStruct(weight.shape, jnp.b...  32.8 us
    unnamed x1, local copies, waits for them, and re-layouts  2.85 us

profile of v4, /device:TPU:0, one launch (start us, length us, event | category | flops | bytes accessed | tf_op | source)
XLA Modules:
  0.0 35.7 jit_solution(813478822521958063)
XLA Ops:
  0.0 32.8 %shard_map.55 = bf16[1,256,3584]{2,1,0:T(8,128)(2,1)} custom-call(bf16[16,3584]{1,0:T(8,128)(2,1)} %tok_hbm.1, s32[8,16]{1,0:T(8,128)} %bitcast.3, bf16[1,256,3584]{2,1,0:T(8,128)(2,1)} %w_hbm.1, s32[112,256]{1,0:T(8,128)} %bitcast.2, f32[1,3584]{1,0:T(1,128)} %damp_hbm.1), custom_call_target="tpu_custom_call" | custom-call | flops 939524096 | bytes 3670016 | tf_op jit(solution)/shard_map/pallas_call | solution.py:271
  32.8 2.8 %copy.7 = bf16[1,256,3584]{2,1,0:T(8,128)(2,1)} copy(bf16[1,256,3584]{2,1,0:T(8,128)(2,1)} %shard_map.55) | data formatting | bytes 3670016

commit v5 on v4

--- a/solution.py
+++ b/solution.py
@@ -76,7 +76,7 @@
 
 def kernel(tok_hbm, ids_hbm, w_hbm, bits_hbm, damp_hbm, out_hbm,
            held, w_ref, pruned, keep, part, other, squares, ids_ref, wide_ids, bits_ref, words, damp_ref, out_ref,
-           load_sem, recv_sem, x_sem, core_sem, line_sem, y_send, y_recv, store_sem):
+           load_sem, recv_sem, x_sem, core_sem, mate_sem, across_sem, y_send, y_recv, store_sem):
     z, cross, y = lax.axis_index("expert"), lax.axis_index("hrow"), lax.axis_index("hcol")
     tok_count, feat = tok_hbm.shape
     slab = w_hbm.shape[1]
@@ -84,12 +84,13 @@
     spans = ((0, half), (half, feat + FLAGS - half))
     x, core = cross // 2, cross % 2
     upper = z // 2
+    inner = (z + 1) // 2 % 2
     mate = 4 * upper + 1 - z
+    across = 3 - z
     order = (z, mate, 2 - upper, 3 - 3 * upper)
     x_row, core_row = (1 - x) * 2 + core, x * 2 + 1 - core
     both_row = (1 - x) * 2 + 1 - core
-    to_mate = (mate, cross, y)
-    to_line = [(order[step], cross, y) for step in (3, 2, 1)]
+    to_mate, to_across = (mate, cross, y), (across, cross, y)
     to_x, to_core, to_y = (z, x_row, y), (z, core_row, y), (z, cross, 1 - y)
     mine = z * 4 + cross
 
@@ -101,8 +102,12 @@
         pltpu.make_async_copy(damp_hbm, damp_ref, load_sem.at[4]),
     ]
     barrier = pltpu.get_barrier_semaphore()
-    for device in to_line + [to_x, to_core, to_y]:
+    for device in (to_mate, to_x, to_core, to_y):
         pl.semaphore_signal(barrier, inc=1, device_id=device, device_id_type=MESH)
+
+    @pl.when(inner == 1)
+    def _():
+        pl.semaphore_signal(barrier, inc=1, device_id=to_across, device_id_type=MESH)
 
     for load in loads:
         load.start()
@@ -117,34 +122,45 @@
     def arrived(number, h):
         block(number, h, x_sem.at[0, 0], to_x).wait_recv()
 
-    always = []
+    always, inners = [], []
 
     def send(number, h, sem, device):
         copy = block(number, h, sem, device)
         copy.start()
         always.append(copy)
 
+    def inward(number, h, sem, device):
+        @pl.when(inner == 1)
+        def _():
+            block(number, h, sem, device).start()
+
+        inners.append(block(number, h, sem, device))
+
     def spread(number, h):
+        inward(number, h, across_sem.at[0, h], to_across)
+        send(number, h, mate_sem.at[0, h], to_mate)
         send(number, h, x_sem.at[0, h], to_x)
-        for place, device in enumerate(to_line):
-            send(number, h, line_sem.at[place, h], device)
         send(number, h, core_sem.at[0, h], to_core)
 
-    def column(step):
+    def column(step, h):
         number = order[step] * 4 + cross
-        for h in (0, 1):
-            arrived(number, h)
-            if not (step == 1 and h == 1):
-                send(number, h, x_sem.at[step, h], to_x)
-            send(number, h, core_sem.at[step, h], to_core)
+        arrived(number, h)
+        if step == 1:
+            inward(number, h, across_sem.at[1, h], to_across)
+        else:
+            inward(number, h, mate_sem.at[step, h], to_mate)
+        if not (step == 1 and h == 1):
+            send(number, h, x_sem.at[step, h], to_x)
+        send(number, h, core_sem.at[step, h], to_core)
 
     def crossed(step):
         number = order[step] * 4 + x_row
         for h in (0, 1):
             arrived(number, h)
-            if step == 0 and h == 1:
-                send(number, h, line_sem.at[3, 0], to_mate)
             send(number, h, core_sem.at[4 + step, h], to_core)
+
+    def around():
+        send(z * 4 + x_row, 1, mate_sem.at[1, 0], to_mate)
 
     def rows_of(first, count):
         return pl.ds(pl.multiple_of(first * tok_count, tok_count), count * tok_count)
@@ -193,7 +209,7 @@
         named = jnp.where(wide_ids[k:k + 1, :] == expert, 1.0, named)
     held[mine, :, feat:feat + FLAGS] = named.T[0:tok_count, :].astype(jnp.bfloat16)
     loads[0].wait()
-    pl.semaphore_wait(barrier, 6)
+    pl.semaphore_wait(barrier, 4 + inner)
 
     for h in (0, 1):
         spread(mine, h)
@@ -219,20 +235,22 @@
         return carry
 
     steps = feat // 128
-    lax.fori_loop(0, steps // 2, unpack, 0)
-    column(1)
+    lax.fori_loop(0, steps, unpack, 0)
+    for h in (0, 1):
+        column(1, h)
+        column(2, h)
     crossed(0)
-    lax.fori_loop(steps // 2, steps, unpack, 0)
-    column(2)
+    column(3, 0)
+    column(3, 1)
+    around()
+    crossed(2)
+    plane(0)
     crossed(1)
-    plane(0)
+    plane(2)
+    crossed(3)
     plane(1)
-    column(3)
-    crossed(2)
-    plane(2)
     other_core(3, core_row)
     project(order[3] * 4 + 2 * x, 2)
-    crossed(3)
     other_core(3, both_row)
     project(order[3] * 4 + 2 * (1 - x), 2)
 
@@ -258,8 +276,25 @@
     for copy in summed:
         copy.wait_send()
 
+    @pl.when(inner == 1)
+    def _():
+        for copy in inners:
+            copy.wait_send()
+
     for store in stores:
         store.wait()
+
+
+def leave(from_hbm, to_hbm, sems):
+    rows = from_hbm.shape[1] // 4
+    copies = []
+    for i in range(4):
+        at = pl.ds(i * rows, rows)
+        copies.append(pltpu.make_async_copy(from_hbm.at[0, at, :], to_hbm.at[0, at, :], sems.at[i]))
+    for copy in copies:
+        copy.start()
+    for copy in copies:
+        copy.wait()
 
 
 def gathered(tokens, expert_ids, weight, mask_bits, damping):
@@ -268,7 +303,7 @@
     blocks = 16
     total = blocks * tok_count
     dma = pltpu.SemaphoreType.DMA
-    return pl.pallas_call(
+    result = pl.pallas_call(
         kernel,
         out_shape=jax.ShapeDtypeStruct(weight.shape, jnp.bfloat16),
         in_specs=[pl.BlockSpec(memory_space=pltpu.HBM)] * 5,
@@ -292,6 +327,7 @@
             dma((4, 2)),
             dma((8, 2)),
             dma((4, 2)),
+            dma((2, 2)),
             dma((5,)),
             dma((5,)),
             dma((feat // WIDE,)),
@@ -301,6 +337,13 @@
         cost_estimate=pl.CostEstimate(
             flops=4 * total * slab * feat, bytes_accessed=4 * slab * feat, transcendentals=0),
     )(tokens, expert_ids.T, weight, mask_bits.T, damping)
+    return pl.pallas_call(
+        leave,
+        out_shape=jax.ShapeDtypeStruct(weight.shape, jnp.bfloat16),
+        in_specs=[pl.BlockSpec(memory_space=pl.ANY)],
+        out_specs=pl.BlockSpec(memory_space=pl.ANY),
+        scratch_shapes=[dma((4,))],
+    )(result)
 
 
 def solution(mesh):

time: 35.8 us -> 85.5 us (2.39)
  Pallas kernels: 32.8 us -> 85.4 us
  local copies, waits for them, and re-layouts: 2.85 us -> 0 us
    pallas_call x0 -> x1, Pallas kernels: none -> 56.7 us  [gathered(): pl.pallas_call(leave, out_shape=jax.ShapeDtypeStruct(weight.shape, jnp.bf...]
    pallas_call x1, Pallas kernels: 32.8 us -> 28.6 us  [gathered(): pl.pallas_call(kernel, out_shape=jax.ShapeDtypeStruct(weight.shape, jnp.b...]
    unnamed x1 -> x0, local copies, waits for them, and re-layouts: 2.85 us -> none
where the time goes in v5:
time: 85.5 us; the launch traced here: 85.4 us
  Pallas kernels  85.4 us (100%)
    pallas_call x1, Pallas kernels, gathered(): pl.pallas_call(leave, out_shape=jax.ShapeDtypeStruct(weight.shape, jnp.bf...  56.7 us
    pallas_call x1, Pallas kernels, gathered(): pl.pallas_call(kernel, out_shape=jax.ShapeDtypeStruct(weight.shape, jnp.b...  28.6 us

profile of v5, /device:TPU:0, one launch (start us, length us, event | category | flops | bytes accessed | tf_op | source)
XLA Modules:
  0.0 85.4 jit_solution(15992678156882447614)
XLA Ops:
  0.0 28.6 %shard_map.55.from_hbm = bf16[1,256,3584]{2,1,0:T(8,128)(2,1)} custom-call(bf16[16,3584]{1,0:T(8,128)(2,1)} %tok_hbm.1, s32[8,16]{1,0:T(8,128)} %bitcast.3, bf16[1,256,3584]{2,1,0:T(8,128)(2,1)} %w_hbm.1, s32[112,256]{1,0:T(8,128)} %bitcast.2, f32[1,3584]{1,0:T(1,128)} %damp_hbm.1), custom_call_target="tpu_custom_call" | custom-call | flops 939524096 | bytes 3670016 | tf_op jit(solution)/shard_map/pallas_call | solution.py:306
  28.6 56.7 %shard_map.56 = bf16[1,256,3584]{2,1,0:T(8,128)(2,1)} custom-call(bf16[1,256,3584]{2,1,0:T(8,128)(2,1)} %shard_map.55.from_hbm), custom_call_target="tpu_custom_call" | custom-call | tf_op jit(solution)/shard_map/pallas_call | solution.py:340

commit v6 on v5

--- a/solution.py
+++ b/solution.py
@@ -72,6 +72,7 @@
 FLAGS = 128
 CHUNK = 256
 WIDE = 512
+PIECES = 4
 
 
 def kernel(tok_hbm, ids_hbm, w_hbm, bits_hbm, damp_hbm, out_hbm,
@@ -80,8 +81,10 @@
     z, cross, y = lax.axis_index("expert"), lax.axis_index("hrow"), lax.axis_index("hcol")
     tok_count, feat = tok_hbm.shape
     slab = w_hbm.shape[1]
-    half = feat // 256 * 128
-    spans = ((0, half), (half, feat + FLAGS - half))
+    quarter = feat // (128 * PIECES) * 128
+    spans = [(i * quarter, quarter) for i in range(PIECES - 1)]
+    spans.append(((PIECES - 1) * quarter, feat + FLAGS - (PIECES - 1) * quarter))
+    whole = (0, feat + FLAGS)
     x, core = cross // 2, cross % 2
     upper = z // 2
     inner = (z + 1) // 2 % 2
@@ -113,10 +116,10 @@
         load.start()
 
     def block(number, h, sem, device):
-        lo, size = spans[h]
+        lo, size = whole if h is None else spans[h]
         piece = held.at[number, :, pl.ds(lo, size)]
         return pltpu.make_async_remote_copy(
-            src_ref=piece, dst_ref=piece, send_sem=sem, recv_sem=recv_sem.at[number, h],
+            src_ref=piece, dst_ref=piece, send_sem=sem, recv_sem=recv_sem.at[number, h or 0],
             device_id=device, device_id_type=MESH)
 
     def arrived(number, h):
@@ -140,7 +143,6 @@
         inward(number, h, across_sem.at[0, h], to_across)
         send(number, h, mate_sem.at[0, h], to_mate)
         send(number, h, x_sem.at[0, h], to_x)
-        send(number, h, core_sem.at[0, h], to_core)
 
     def column(step, h):
         number = order[step] * 4 + cross
@@ -149,18 +151,16 @@
             inward(number, h, across_sem.at[1, h], to_across)
         else:
             inward(number, h, mate_sem.at[step, h], to_mate)
-        if not (step == 1 and h == 1):
-            send(number, h, x_sem.at[step, h], to_x)
-        send(number, h, core_sem.at[step, h], to_core)
+        send(number, h, x_sem.at[step, h], to_x)
+
+    def to_other_core(step):
+        send(order[step] * 4 + cross, None, core_sem.at[step], to_core)
 
     def crossed(step):
         number = order[step] * 4 + x_row
-        for h in (0, 1):
+        for h in range(PIECES):
             arrived(number, h)
-            send(number, h, core_sem.at[4 + step, h], to_core)
-
-    def around():
-        send(z * 4 + x_row, 1, mate_sem.at[1, 0], to_mate)
+        send(number, None, core_sem.at[4 + step], to_core)
 
     def rows_of(first, count):
         return pl.ds(pl.multiple_of(first * tok_count, tok_count), count * tok_count)
@@ -192,8 +192,7 @@
             squares[:, lo:lo + CHUNK] = total if len(summed) == 1 else squares[:, lo:lo + CHUNK] + total
 
     def other_core(step, row):
-        for h in (0, 1):
-            arrived(order[step] * 4 + row, h)
+        arrived(order[step] * 4 + row, None)
 
     def plane(step):
         other_core(step, core_row)
@@ -211,8 +210,9 @@
     loads[0].wait()
     pl.semaphore_wait(barrier, 4 + inner)
 
-    for h in (0, 1):
+    for h in range(PIECES):
         spread(mine, h)
+    to_other_core(0)
 
     filled = bits_hbm.shape[0]
     if filled < 128:
@@ -236,19 +236,21 @@
 
     steps = feat // 128
     lax.fori_loop(0, steps, unpack, 0)
-    for h in (0, 1):
+    for h in range(PIECES):
         column(1, h)
         column(2, h)
+    to_other_core(1)
+    to_other_core(2)
     crossed(0)
-    column(3, 0)
-    column(3, 1)
-    around()
+    for h in range(PIECES):
+        column(3, h)
+    to_other_core(3)
+    crossed(1)
     crossed(2)
     plane(0)
-    crossed(1)
+    plane(1)
+    crossed(3)
     plane(2)
-    crossed(3)
-    plane(1)
     other_core(3, core_row)
     project(order[3] * 4 + 2 * x, 2)
     other_core(3, both_row)
@@ -285,16 +287,19 @@
         store.wait()
 
 
-def leave(from_hbm, to_hbm, sems):
-    rows = from_hbm.shape[1] // 4
-    copies = []
-    for i in range(4):
+def leave(from_hbm, to_hbm, slabs, in_sems, out_sems):
+    count, rows = slabs.shape[0], slabs.shape[1]
+    ins, outs = [], []
+    for i in range(count):
         at = pl.ds(i * rows, rows)
-        copies.append(pltpu.make_async_copy(from_hbm.at[0, at, :], to_hbm.at[0, at, :], sems.at[i]))
-    for copy in copies:
-        copy.start()
-    for copy in copies:
-        copy.wait()
+        ins.append(pltpu.make_async_copy(from_hbm.at[0, at, :], slabs.at[i], in_sems.at[i]))
+        outs.append(pltpu.make_async_copy(slabs.at[i], to_hbm.at[0, at, :], out_sems.at[i]))
+        ins[i].start()
+    for i in range(count):
+        ins[i].wait()
+        outs[i].start()
+    for out in outs:
+        out.wait()
 
 
 def gathered(tokens, expert_ids, weight, mask_bits, damping):
@@ -323,11 +328,11 @@
             pltpu.VMEM((1, feat), jnp.float32),
             pltpu.VMEM((slab, feat), jnp.bfloat16),
             dma((5,)),
-            dma((blocks, 2)),
-            dma((4, 2)),
-            dma((8, 2)),
-            dma((4, 2)),
-            dma((2, 2)),
+            dma((blocks, PIECES)),
+            dma((4, PIECES)),
+            dma((8,)),
+            dma((4, PIECES)),
+            dma((2, PIECES)),
             dma((5,)),
             dma((5,)),
             dma((feat // WIDE,)),
@@ -342,7 +347,8 @@
         out_shape=jax.ShapeDtypeStruct(weight.shape, jnp.bfloat16),
         in_specs=[pl.BlockSpec(memory_space=pl.ANY)],
         out_specs=pl.BlockSpec(memory_space=pl.ANY),
-        scratch_shapes=[dma((4,))],
+        scratch_shapes=[pltpu.VMEM((8, slab // 8, feat), jnp.bfloat16), dma((8,)), dma((8,))],
+        compiler_params=pltpu.CompilerParams(vmem_limit_bytes=62 * 1024 * 1024),
     )(result)
 
 

time: 85.5 us -> 32.3 us (0.38)
  Pallas kernels: 85.4 us -> 32.2 us
    pallas_call x1, Pallas kernels: 56.7 us -> 2.41 us  [gathered(): pl.pallas_call(leave, out_shape=jax.ShapeDtypeStruct(weight.shape, jnp.bf...]
    pallas_call x1, Pallas kernels: 28.6 us -> 29.8 us  [gathered(): pl.pallas_call(kernel, out_shape=jax.ShapeDtypeStruct(weight.shape, jnp.b...]
where the time goes in v6:
time: 32.3 us; the launch traced here: 32.2 us
  Pallas kernels  32.2 us (100%)
    pallas_call x1, Pallas kernels, gathered(): pl.pallas_call(kernel, out_shape=jax.ShapeDtypeStruct(weight.shape, jnp.b...  29.8 us
    pallas_call x1, Pallas kernels, gathered(): pl.pallas_call(leave, out_shape=jax.ShapeDtypeStruct(weight.shape, jnp.bf...  2.41 us

profile of v6, /device:TPU:0, one launch (start us, length us, event | category | flops | bytes accessed | tf_op | source)
XLA Modules:
  0.0 32.2 jit_solution(17899733112305297111)
XLA Ops:
  0.0 29.8 %shard_map.55.from_hbm = bf16[1,256,3584]{2,1,0:T(8,128)(2,1)} custom-call(bf16[16,3584]{1,0:T(8,128)(2,1)} %tok_hbm.1, s32[8,16]{1,0:T(8,128)} %bitcast.3, bf16[1,256,3584]{2,1,0:T(8,128)(2,1)} %w_hbm.1, s32[112,256]{1,0:T(8,128)} %bitcast.2, f32[1,3584]{1,0:T(1,128)} %damp_hbm.1), custom_call_target="tpu_custom_call" | custom-call | flops 939524096 | bytes 3670016 | tf_op jit(solution)/shard_map/pallas_call | solution.py:311
  29.8 2.4 %shard_map.56 = bf16[1,256,3584]{2,1,0:T(8,128)(2,1)} custom-call(bf16[1,256,3584]{2,1,0:T(8,128)(2,1)} %shard_map.55.from_hbm), custom_call_target="tpu_custom_call" | custom-call | tf_op jit(solution)/shard_map/pallas_call | solution.py:345

commit v7 on v6

--- a/solution.py
+++ b/solution.py
@@ -125,42 +125,51 @@
     def arrived(number, h):
         block(number, h, x_sem.at[0, 0], to_x).wait_recv()
 
-    always, inners = [], []
-
-    def send(number, h, sem, device):
-        copy = block(number, h, sem, device)
-        copy.start()
-        always.append(copy)
-
-    def inward(number, h, sem, device):
-        @pl.when(inner == 1)
+    sent = {None: [], 0: [], 1: []}
+    own_column = [order[step] * 4 + cross for step in range(4)]
+    other_column = [order[step] * 4 + x_row for step in range(4)]
+
+    def send(number, h, sem, at, device, where=None):
+        block(number, h, sem.at[at], device).start()
+        sent[where].append((number, h, sem, at, device))
+
+    def send_on(kind, number, h, sem, at, device):
+        @pl.when(inner == kind)
         def _():
-            block(number, h, sem, device).start()
-
-        inners.append(block(number, h, sem, device))
-
-    def spread(number, h):
-        inward(number, h, across_sem.at[0, h], to_across)
-        send(number, h, mate_sem.at[0, h], to_mate)
-        send(number, h, x_sem.at[0, h], to_x)
-
-    def column(step, h):
-        number = order[step] * 4 + cross
+            send(number, h, sem, at, device, kind)
+
+    def finish(where):
+        for number, h, sem, at, device in sent[where]:
+            block(number, h, sem.at[at], device).wait_send()
+
+    def spread(h):
+        send_on(1, mine, h, across_sem, (0, h), to_across)
+        send(mine, h, mate_sem, (0, h), to_mate)
+        send(mine, h, x_sem, (0, h), to_x)
+
+    def column(step, h, where=None):
+        number = own_column[step]
         arrived(number, h)
-        if step == 1:
-            inward(number, h, across_sem.at[1, h], to_across)
-        else:
-            inward(number, h, mate_sem.at[step, h], to_mate)
-        send(number, h, x_sem.at[step, h], to_x)
+        if where != 0:
+            sem, device = (across_sem, to_across) if step == 1 else (mate_sem, to_mate)
+            at = (1, h) if step == 1 else (step, h)
+            if where == 1:
+                send(number, h, sem, at, device, 1)
+            else:
+                send_on(1, number, h, sem, at, device)
+        if step > 1 or (where == 0 and h < PIECES // 2):
+            send(number, h, x_sem, (step, h), to_x, where)
 
     def to_other_core(step):
-        send(order[step] * 4 + cross, None, core_sem.at[step], to_core)
+        send(own_column[step], None, core_sem, (step, 0), to_core)
 
     def crossed(step):
-        number = order[step] * 4 + x_row
         for h in range(PIECES):
-            arrived(number, h)
-        send(number, None, core_sem.at[4 + step], to_core)
+            arrived(other_column[step], h)
+            if step == 3:
+                send(other_column[step], h, core_sem, (4 + step, h), to_core)
+        if step < 3:
+            send(other_column[step], None, core_sem, (4 + step, 0), to_core)
 
     def rows_of(first, count):
         return pl.ds(pl.multiple_of(first * tok_count, tok_count), count * tok_count)
@@ -192,7 +201,8 @@
             squares[:, lo:lo + CHUNK] = total if len(summed) == 1 else squares[:, lo:lo + CHUNK] + total
 
     def other_core(step, row):
-        arrived(order[step] * 4 + row, None)
+        for h in range(PIECES) if step == 3 and row is both_row else (None,):
+            arrived(order[step] * 4 + row, h)
 
     def plane(step):
         other_core(step, core_row)
@@ -211,7 +221,7 @@
     pl.semaphore_wait(barrier, 4 + inner)
 
     for h in range(PIECES):
-        spread(mine, h)
+        spread(h)
     to_other_core(0)
 
     filled = bits_hbm.shape[0]
@@ -236,14 +246,30 @@
 
     steps = feat // 128
     lax.fori_loop(0, steps, unpack, 0)
-    for h in range(PIECES):
-        column(1, h)
-        column(2, h)
+    @pl.when(inner == 1)
+    def _():
+        for h in range(PIECES):
+            column(1, h, 1)
+            column(2, h, 1)
+        for h in range(PIECES):
+            arrived(other_column[0], h)
+
+    @pl.when(inner == 0)
+    def _():
+        for h in range(PIECES):
+            column(1, h, 0)
+            arrived(other_column[0], h)
+            send(other_column[0], h, mate_sem, (1, h), to_mate, 0)
+        for h in range(PIECES):
+            column(2, h, 0)
+
     to_other_core(1)
     to_other_core(2)
-    crossed(0)
+    send(other_column[0], None, core_sem, (4, 0), to_core)
     for h in range(PIECES):
         column(3, h)
+    for h in range(PIECES // 2, PIECES):
+        send_on(1, other_column[0], h, mate_sem, (1, h), to_mate)
     to_other_core(3)
     crossed(1)
     crossed(2)
@@ -273,15 +299,17 @@
         store.start()
         stores.append(store)
 
-    for copy in always:
-        copy.wait_send()
+    finish(None)
     for copy in summed:
         copy.wait_send()
 
     @pl.when(inner == 1)
     def _():
-        for copy in inners:
-            copy.wait_send()
+        finish(1)
+
+    @pl.when(inner == 0)
+    def _():
+        finish(0)
 
     for store in stores:
         store.wait()
@@ -330,7 +358,7 @@
             dma((5,)),
             dma((blocks, PIECES)),
             dma((4, PIECES)),
-            dma((8,)),
+            dma((8, PIECES)),
             dma((4, PIECES)),
             dma((2, PIECES)),
             dma((5,)),

time: 32.3 us -> 31.4 us (0.972)
  Pallas kernels: 32.2 us -> 31.2 us
    pallas_call x1, Pallas kernels: 29.8 us -> 28.8 us  [gathered(): pl.pallas_call(kernel, out_shape=jax.ShapeDtypeStruct(weight.shape, jnp.b...]
where the time goes in v7:
time: 31.4 us; the launch traced here: 31.2 us
  Pallas kernels  31.2 us (99%)
    pallas_call x1, Pallas kernels, gathered(): pl.pallas_call(kernel, out_shape=jax.ShapeDtypeStruct(weight.shape, jnp.b...  28.8 us
    pallas_call x1, Pallas kernels, gathered(): pl.pallas_call(leave, out_shape=jax.ShapeDtypeStruct(weight.shape, jnp.bf...  2.41 us

profile of v7, /device:TPU:0, one launch (start us, length us, event | category | flops | bytes accessed | tf_op | source)
XLA Modules:
  0.0 31.2 jit_solution(16691968885578062640)
XLA Ops:
  0.0 28.8 %shard_map.55.from_hbm = bf16[1,256,3584]{2,1,0:T(8,128)(2,1)} custom-call(bf16[16,3584]{1,0:T(8,128)(2,1)} %tok_hbm.1, s32[8,16]{1,0:T(8,128)} %bitcast.3, bf16[1,256,3584]{2,1,0:T(8,128)(2,1)} %w_hbm.1, s32[112,256]{1,0:T(8,128)} %bitcast.2, f32[1,3584]{1,0:T(1,128)} %damp_hbm.1), custom_call_target="tpu_custom_call" | custom-call | flops 939524096 | bytes 3670016 | tf_op jit(solution)/shard_map/pallas_call | solution.py:339
  28.8 2.4 %shard_map.56 = bf16[1,256,3584]{2,1,0:T(8,128)(2,1)} custom-call(bf16[1,256,3584]{2,1,0:T(8,128)(2,1)} %shard_map.55.from_hbm), custom_call_target="tpu_custom_call" | custom-call | tf_op jit(solution)/shard_map/pallas_call | solution.py:373

commit v8 on v7

--- a/solution.py
+++ b/solution.py
@@ -144,7 +144,10 @@
 
     def spread(h):
         send_on(1, mine, h, across_sem, (0, h), to_across)
-        send(mine, h, mate_sem, (0, h), to_mate)
+        if h < PIECES // 2:
+            send(mine, h, mate_sem, (0, h), to_mate)
+        else:
+            send_on(0, mine, h, mate_sem, (0, h), to_mate)
         send(mine, h, x_sem, (0, h), to_x)
 
     def column(step, h, where=None):
@@ -257,30 +260,40 @@
     @pl.when(inner == 0)
     def _():
         for h in range(PIECES):
-            column(1, h, 0)
+            if h < PIECES // 2:
+                column(1, h, 0)
             arrived(other_column[0], h)
             send(other_column[0], h, mate_sem, (1, h), to_mate, 0)
         for h in range(PIECES):
             column(2, h, 0)
 
-    to_other_core(1)
     to_other_core(2)
     send(other_column[0], None, core_sem, (4, 0), to_core)
     for h in range(PIECES):
         column(3, h)
     for h in range(PIECES // 2, PIECES):
+        send_on(1, mine, h, mate_sem, (0, h), to_mate)
+    for h in range(PIECES // 2, PIECES):
         send_on(1, other_column[0], h, mate_sem, (1, h), to_mate)
     to_other_core(3)
-    crossed(1)
     crossed(2)
     plane(0)
-    plane(1)
+
+    @pl.when(inner == 0)
+    def _():
+        for h in range(PIECES // 2, PIECES):
+            arrived(own_column[1], h)
+
+    to_other_core(1)
     crossed(3)
     plane(2)
-    other_core(3, core_row)
-    project(order[3] * 4 + 2 * x, 2)
-    other_core(3, both_row)
-    project(order[3] * 4 + 2 * (1 - x), 2)
+    crossed(1)
+    for step in (3, 1):
+        other_core(step, core_row)
+        project(order[step] * 4 + 2 * x, 2)
+    for step in (3, 1):
+        other_core(step, both_row)
+        project(order[step] * 4 + 2 * (1 - x), 2)
 
     loads[4].wait()
     here = member(held[:, :, feat:feat + FLAGS].reshape(-1, FLAGS))
@@ -361,8 +374,8 @@
             dma((8, PIECES)),
             dma((4, PIECES)),
             dma((2, PIECES)),
-            dma((5,)),
-            dma((5,)),
+            dma((6,)),
+            dma((6,)),
             dma((feat // WIDE,)),
         ],
         compiler_params=pltpu.CompilerParams(

time: 31.4 us -> 34.1 us (1.086)
  Pallas kernels: 31.2 us -> 33.9 us
    pallas_call x1, Pallas kernels: 28.8 us -> 31.5 us  [gathered(): pl.pallas_call(kernel, out_shape=jax.ShapeDtypeStruct(weight.shape, jnp.b...]
where the time goes in v8:
time: 34.1 us; the launch traced here: 34 us
  Pallas kernels  33.9 us (99%)
    pallas_call x1, Pallas kernels, gathered(): pl.pallas_call(kernel, out_shape=jax.ShapeDtypeStruct(weight.shape, jnp.b...  31.5 us
    pallas_call x1, Pallas kernels, gathered(): pl.pallas_call(leave, out_shape=jax.ShapeDtypeStruct(weight.shape, jnp.bf...  2.41 us

profile of v8, /device:TPU:0, one launch (start us, length us, event | category | flops | bytes accessed | tf_op | source)
XLA Modules:
  0.0 34.0 jit_solution(12925576694479871911)
XLA Ops:
  0.0 31.5 %shard_map.55.from_hbm = bf16[1,256,3584]{2,1,0:T(8,128)(2,1)} custom-call(bf16[16,3584]{1,0:T(8,128)(2,1)} %tok_hbm.1, s32[8,16]{1,0:T(8,128)} %bitcast.3, bf16[1,256,3584]{2,1,0:T(8,128)(2,1)} %w_hbm.1, s32[112,256]{1,0:T(8,128)} %bitcast.2, f32[1,3584]{1,0:T(1,128)} %damp_hbm.1), custom_call_target="tpu_custom_call" | custom-call | flops 939524096 | bytes 3670016 | tf_op jit(solution)/shard_map/pallas_call | solution.py:352
  31.5 2.4 %shard_map.56 = bf16[1,256,3584]{2,1,0:T(8,128)(2,1)} custom-call(bf16[1,256,3584]{2,1,0:T(8,128)(2,1)} %shard_map.55.from_hbm), custom_call_target="tpu_custom_call" | custom-call | tf_op jit(solution)/shard_map/pallas_call | solution.py:386

commit v9 on v7

--- a/solution.py
+++ b/solution.py
@@ -75,8 +75,8 @@
 PIECES = 4
 
 
-def kernel(tok_hbm, ids_hbm, w_hbm, bits_hbm, damp_hbm, out_hbm,
-           held, w_ref, pruned, keep, part, other, squares, ids_ref, wide_ids, bits_ref, words, damp_ref, out_ref,
+def kernel(tok_hbm, ids_hbm, w_hbm, bits_hbm, damp_hbm, proj_hbm, scale_hbm, keep_hbm, rows_hbm,
+           held, w_ref, pruned, keep, part, other, squares, ids_ref, wide_ids, bits_ref, words, damp_ref, proj_ref, scale_ref,
            load_sem, recv_sem, x_sem, core_sem, mate_sem, across_sem, y_send, y_recv, store_sem):
     z, cross, y = lax.axis_index("expert"), lax.axis_index("hrow"), lax.axis_index("hcol")
     tok_count, feat = tok_hbm.shape
@@ -184,7 +184,12 @@
         lane = lax.broadcasted_iota(jnp.int32, flags.shape, 1)
         return jnp.sum(jnp.where(lane == mine, flags.astype(jnp.float32), 0.0), axis=1, keepdims=True)
 
-    summed = []
+    summed, stores = [], []
+
+    def store(src, dst):
+        copy = pltpu.make_async_copy(src, dst, store_sem.at[len(stores)])
+        copy.start()
+        stores.append(copy)
 
     def project(first, count):
         rows, blocks = count * tok_count, pl.ds(first, count)
@@ -194,6 +199,7 @@
         copy = y_copy(first, count, len(summed))
         copy.start()
         summed.append(copy)
+        store(held.at[blocks, :, pl.ds(0, feat)], rows_hbm.at[blocks])
         here = member(held[blocks, :, feat:feat + FLAGS].reshape(rows, FLAGS))
         for lo in range(0, feat, CHUNK):
             piece = held[blocks, :, lo:lo + CHUNK].reshape(rows, CHUNK).astype(jnp.float32)
@@ -246,6 +252,7 @@
 
     steps = feat // 128
     lax.fori_loop(0, steps, unpack, 0)
+    store(keep, keep_hbm)
     @pl.when(inner == 1)
     def _():
         for h in range(PIECES):
@@ -283,22 +290,15 @@
     project(order[3] * 4 + 2 * (1 - x), 2)
 
     loads[4].wait()
+    diag = jnp.sum(squares[...], axis=0, keepdims=True) / ROWS_E + damp_ref[...]
+    scale_ref[...] = ETA / ROWS_E / diag
+    store(scale_ref, scale_hbm)
     here = member(held[:, :, feat:feat + FLAGS].reshape(-1, FLAGS))
     for copy in summed:
         copy.wait_recv()
     projected = jnp.where(here > 0.5, part[...] + other[...], 0.0).T.astype(jnp.bfloat16)
-    stores = []
-    for lo in range(0, feat, WIDE):
-        at = slice(lo, lo + WIDE)
-        routed = held[:, :, at].reshape(-1, WIDE)
-        comp = jnp.dot(projected, routed, preferred_element_type=jnp.float32)
-        diag = jnp.sum(squares[:, at], axis=0, keepdims=True) / ROWS_E + damp_ref[:, at]
-        updated = w_ref[:, at].astype(jnp.float32) + comp * (ETA / ROWS_E / diag)
-        out_ref[:, at] = updated.astype(jnp.bfloat16) * keep[:, at]
-        store = pltpu.make_async_copy(out_ref.at[:, at], out_hbm.at[0, :, at], store_sem.at[lo // WIDE])
-        store.start()
-        stores.append(store)
-
+    proj_ref[...] = projected
+    store(proj_ref, proj_hbm)
     finish(None)
     for copy in summed:
         copy.wait_send()
@@ -311,23 +311,43 @@
     def _():
         finish(0)
 
-    for store in stores:
-        store.wait()
-
-
-def leave(from_hbm, to_hbm, slabs, in_sems, out_sems):
-    count, rows = slabs.shape[0], slabs.shape[1]
-    ins, outs = [], []
-    for i in range(count):
-        at = pl.ds(i * rows, rows)
-        ins.append(pltpu.make_async_copy(from_hbm.at[0, at, :], slabs.at[i], in_sems.at[i]))
-        outs.append(pltpu.make_async_copy(slabs.at[i], to_hbm.at[0, at, :], out_sems.at[i]))
-        ins[i].start()
-    for i in range(count):
-        ins[i].wait()
-        outs[i].start()
-    for out in outs:
-        out.wait()
+    for copy in stores:
+        copy.wait()
+
+
+def compensate(proj_hbm, scale_hbm, keep_hbm, rows_hbm, w_hbm, out_hbm,
+               proj_ref, scale_ref, keep, rows, w_ref, out_ref, head_sem, load_sem, store_sem):
+    feat = rows_hbm.shape[1]
+    heads = [
+        pltpu.make_async_copy(proj_hbm, proj_ref, head_sem.at[0]),
+        pltpu.make_async_copy(scale_hbm, scale_ref, head_sem.at[1]),
+    ]
+    for copy in heads:
+        copy.start()
+    loads, stores = [], []
+    for i in range(feat // WIDE):
+        at = slice(i * WIDE, (i + 1) * WIDE)
+        loads.append([
+            pltpu.make_async_copy(rows_hbm.at[:, at], rows.at[:, at], load_sem.at[i, 0]),
+            pltpu.make_async_copy(w_hbm.at[0, :, at], w_ref.at[:, at], load_sem.at[i, 1]),
+            pltpu.make_async_copy(keep_hbm.at[:, at], keep.at[:, at], load_sem.at[i, 2]),
+        ])
+        for copy in loads[i]:
+            copy.start()
+    for copy in heads:
+        copy.wait()
+    for i in range(feat // WIDE):
+        at = slice(i * WIDE, (i + 1) * WIDE)
+        for copy in loads[i]:
+            copy.wait()
+        comp = jnp.dot(proj_ref[...], rows[:, at], preferred_element_type=jnp.float32)
+        updated = w_ref[:, at].astype(jnp.float32) + comp * scale_ref[:, at]
+        out_ref[:, at] = updated.astype(jnp.bfloat16) * keep[:, at]
+        copy = pltpu.make_async_copy(out_ref.at[:, at], out_hbm.at[0, :, at], store_sem.at[i])
+        copy.start()
+        stores.append(copy)
+    for copy in stores:
+        copy.wait()
 
 
 def gathered(tokens, expert_ids, weight, mask_bits, damping):
@@ -336,11 +356,16 @@
     blocks = 16
     total = blocks * tok_count
     dma = pltpu.SemaphoreType.DMA
-    result = pl.pallas_call(
+    projected, scale, keep, rows = pl.pallas_call(
         kernel,
-        out_shape=jax.ShapeDtypeStruct(weight.shape, jnp.bfloat16),
+        out_shape=[
+            jax.ShapeDtypeStruct((slab, total), jnp.bfloat16),
+            jax.ShapeDtypeStruct((1, feat), jnp.float32),
+            jax.ShapeDtypeStruct((slab, feat), jnp.bfloat16),
+            jax.ShapeDtypeStruct((blocks, tok_count, feat), jnp.bfloat16),
+        ],
         in_specs=[pl.BlockSpec(memory_space=pltpu.HBM)] * 5,
-        out_specs=pl.BlockSpec(memory_space=pl.ANY),
+        out_specs=[pl.BlockSpec(memory_space=pl.ANY)] * 4,
         scratch_shapes=[
             pltpu.VMEM((blocks, tok_count, feat + FLAGS), jnp.bfloat16),
             pltpu.VMEM((slab, feat), jnp.bfloat16),
@@ -354,7 +379,8 @@
             pltpu.VMEM((128, slab), jnp.int32),
             pltpu.VMEM((slab, 128), jnp.int32),
             pltpu.VMEM((1, feat), jnp.float32),
-            pltpu.VMEM((slab, feat), jnp.bfloat16),
+            pltpu.VMEM((slab, total), jnp.bfloat16),
+            pltpu.VMEM((1, feat), jnp.float32),
             dma((5,)),
             dma((blocks, PIECES)),
             dma((4, PIECES)),
@@ -363,21 +389,26 @@
             dma((2, PIECES)),
             dma((5,)),
             dma((5,)),
-            dma((feat // WIDE,)),
+            dma((8,)),
         ],
         compiler_params=pltpu.CompilerParams(
             collective_id=0, has_side_effects=True, vmem_limit_bytes=62 * 1024 * 1024),
         cost_estimate=pl.CostEstimate(
             flops=4 * total * slab * feat, bytes_accessed=4 * slab * feat, transcendentals=0),
     )(tokens, expert_ids.T, weight, mask_bits.T, damping)
+    spare = pltpu.VMEM((slab, feat), jnp.bfloat16)
     return pl.pallas_call(
-        leave,
+        compensate,
         out_shape=jax.ShapeDtypeStruct(weight.shape, jnp.bfloat16),
-        in_specs=[pl.BlockSpec(memory_space=pl.ANY)],
+        in_specs=[pl.BlockSpec(memory_space=pltpu.HBM)] * 5,
         out_specs=pl.BlockSpec(memory_space=pl.ANY),
-        scratch_shapes=[pltpu.VMEM((8, slab // 8, feat), jnp.bfloat16), dma((8,)), dma((8,))],
+        scratch_shapes=[
+            pltpu.VMEM((slab, total), jnp.bfloat16), pltpu.VMEM((1, feat), jnp.float32), spare,
+            pltpu.VMEM((total, feat), jnp.bfloat16), spare, spare,
+            dma((2,)), dma((feat // WIDE, 3)), dma((feat // WIDE,)),
+        ],
         compiler_params=pltpu.CompilerParams(vmem_limit_bytes=62 * 1024 * 1024),
-    )(result)
+    )(projected, scale, keep, rows.reshape(total, feat), weight)
 
 
 def solution(mesh):

time: 31.4 us -> 33 us (1.051)
  Pallas kernels: 31.2 us -> 32.8 us
    pallas_call x2, Pallas kernels: 31.2 us -> 32.8 us  [the longest x1 27.7 us: gathered(): pl.pallas_call(kernel, out_shape=[jax.ShapeDtypeStruct((slab, total), jnp...]
where the time goes in v9:
time: 33 us; the launch traced here: 32.8 us
  Pallas kernels  32.8 us (99%)
    pallas_call x1, Pallas kernels, gathered(): pl.pallas_call(kernel, out_shape=[jax.ShapeDtypeStruct((slab, total), jnp...  27.7 us
    pallas_call x1, Pallas kernels, gathered(): pl.pallas_call(compensate, out_shape=jax.ShapeDtypeStruct(weight.shape, j...  5.11 us

profile of v9, /device:TPU:0, one launch (start us, length us, event | category | flops | bytes accessed | tf_op | source)
XLA Modules:
  0.0 32.8 jit_solution(10526004502020692065)
XLA Ops:
  0.0 27.7 %shard_map.55 = (bf16[256,256]{1,0:T(8,128)(2,1)}, f32[1,3584]{1,0:T(1,128)}, bf16[256,3584]{1,0:T(8,128)(2,1)}, bf16[16,16,3584]{2,1,0:T(8,128)(2,1)}) custom-call(bf16[16,3584]{1,0:T(8,128)(2,1)} %tok_hbm.1, s32[8,16]{1,0:T(8,128)} %bitcast.5, bf16[1,256,3584]{2,1,0:T(8,128)(2,1)} %w_hbm.3, s32[112,256]{1,0:T(8,128)} %bitcast.4, f32[1,3584]{1,0:T(1,128)} %damp_hbm.1), custom_call_target="tpu_custom_call" | custom-call | flops 939524096 | bytes 3670016 | tf_op jit(solution)/shard_map/pallas_call | solution.py:359
  27.7 5.1 %shard_map.56 = bf16[1,256,3584]{2,1,0:T(8,128)(2,1)} custom-call(bf16[256,256]{1,0:T(8,128)(2,1)} %get-tuple-element.9.proj_hbm, f32[1,3584]{1,0:T(1,128)} %get-tuple-element.10.scale_hbm, bf16[256,3584]{1,0:T(8,128)(2,1)} %get-tuple-element.11.keep_hbm, bf16[256,3584]{1,0:T(8,128)(2,1)} %bitcast.3, bf16[1,256,3584]{2,1,0:T(8,128)(2,1)} %w_hbm.3), custom_call_target="tpu_custom_call" | custom-call | tf_op jit(solution)/shard_map/pallas_call | solution.py:400

commit v10 on v7

--- a/solution.py
+++ b/solution.py
@@ -271,14 +271,14 @@
     for h in range(PIECES // 2, PIECES):
         send_on(1, other_column[0], h, mate_sem, (1, h), to_mate)
     to_other_core(3)
-    crossed(1)
     crossed(2)
     plane(0)
-    plane(1)
     crossed(3)
+    crossed(1)
     plane(2)
     other_core(3, core_row)
     project(order[3] * 4 + 2 * x, 2)
+    plane(1)
     other_core(3, both_row)
     project(order[3] * 4 + 2 * (1 - x), 2)
 

time: 31.4 us -> 32.7 us (1.041)
  Pallas kernels: 31.2 us -> 32.5 us
    pallas_call x1, Pallas kernels: 28.8 us -> 30.1 us  [gathered(): pl.pallas_call(kernel, out_shape=jax.ShapeDtypeStruct(weight.shape, jnp.b...]
where the time goes in v10:
time: 32.7 us; the launch traced here: 32.5 us
  Pallas kernels  32.5 us (99%)
    pallas_call x1, Pallas kernels, gathered(): pl.pallas_call(kernel, out_shape=jax.ShapeDtypeStruct(weight.shape, jnp.b...  30.1 us
    pallas_call x1, Pallas kernels, gathered(): pl.pallas_call(leave, out_shape=jax.ShapeDtypeStruct(weight.shape, jnp.bf...  2.41 us

profile of v10, /device:TPU:0, one launch (start us, length us, event | category | flops | bytes accessed | tf_op | source)
XLA Modules:
  0.0 32.5 jit_solution(1573384954384311758)
XLA Ops:
  0.0 30.1 %shard_map.55.from_hbm = bf16[1,256,3584]{2,1,0:T(8,128)(2,1)} custom-call(bf16[16,3584]{1,0:T(8,128)(2,1)} %tok_hbm.1, s32[8,16]{1,0:T(8,128)} %bitcast.3, bf16[1,256,3584]{2,1,0:T(8,128)(2,1)} %w_hbm.1, s32[112,256]{1,0:T(8,128)} %bitcast.2, f32[1,3584]{1,0:T(1,128)} %damp_hbm.1), custom_call_target="tpu_custom_call" | custom-call | flops 939524096 | bytes 3670016 | tf_op jit(solution)/shard_map/pallas_call | solution.py:339
  30.1 2.4 %shard_map.56 = bf16[1,256,3584]{2,1,0:T(8,128)(2,1)} custom-call(bf16[1,256,3584]{2,1,0:T(8,128)(2,1)} %shard_map.55.from_hbm), custom_call_target="tpu_custom_call" | custom-call | tf_op jit(solution)/shard_map/pallas_call | solution.py:373
